TPU v7x, 32 devices: a whole 2x2x4 slice. The times are simulated.
32 devices in a mesh: dp: 2 (over y), ctx: 16 (over z, x, core).
Axes of the slice: x: 2, y: 2, z: 4, core: 2. Of those that a mesh axis runs over, the one named last changes fastest.
Arguments:
- hidden_in: bfloat16 [4, 1024, 1024], P('dp', 'ctx'), may hold values from -6 to 6
- out_cotangent: bfloat16 [4, 1024, 1024], P('dp', 'ctx'), may hold values from -6 to 6
- attn_gain: bfloat16 [1024], P(('dp', 'ctx')), may hold values from 0.5 to 1.5
- attn_shift: bfloat16 [1024], P(('dp', 'ctx')), may hold values from -3 to 3
- qkv_weight: bfloat16 [1024, 3072], P(('dp', 'ctx')), may hold values from -1 to 1
- qkv_bias: bfloat16 [3072], P(('dp', 'ctx')), may hold values from -2 to 2
- proj_weight: bfloat16 [1024, 1024], P(('dp', 'ctx')), may hold values from -1.5 to 1.5
- proj_bias: bfloat16 [1024], P(('dp', 'ctx')), may hold values from -2 to 2
- mlp_gain: bfloat16 [1024], P(('dp', 'ctx')), may hold values from 0.5 to 1.5
- mlp_shift: bfloat16 [1024], P(('dp', 'ctx')), may hold values from -3 to 3
- up_weight: bfloat16 [1024, 4096], P(('dp', 'ctx')), may hold values from -0.1875 to 0.1875
- up_bias: bfloat16 [4096], P(('dp', 'ctx')), may hold values from -3 to 3
- down_weight: bfloat16 [4096, 1024], P(('dp', 'ctx')), may hold values from -0.09375 to 0.09375
- down_bias: bfloat16 [1024], P(('dp', 'ctx')), may hold values from -2 to 2
- picture_starts: int32 [4, 4], P('dp'), may hold values from 0 to 768, as said below
- group_order: int32 [16], replicated, may hold values from 0 to 15, each once
Outputs:
- block_out: bfloat16 [4, 1024, 1024], P('dp', 'ctx')
- grad_hidden: bfloat16 [4, 1024, 1024], P('dp', 'ctx')
- grad_attn_gain: float32 [1024], P(('dp', 'ctx'))
- grad_attn_shift: float32 [1024], P(('dp', 'ctx'))
- grad_qkv_weight: float32 [1024, 3072], P(('dp', 'ctx'))
- grad_qkv_bias: float32 [3072], P(('dp', 'ctx'))
- grad_proj_weight: float32 [1024, 1024], P(('dp', 'ctx'))
- grad_proj_bias: float32 [1024], P(('dp', 'ctx'))
- grad_mlp_gain: float32 [1024], P(('dp', 'ctx'))
- grad_mlp_shift: float32 [1024], P(('dp', 'ctx'))
- grad_up_weight: float32 [1024, 4096], P(('dp', 'ctx'))
- grad_up_bias: float32 [4096], P(('dp', 'ctx'))
- grad_down_weight: float32 [4096, 1024], P(('dp', 'ctx'))
- grad_down_bias: float32 [1024], P(('dp', 'ctx'))
- clipped_qkv: float32 [1024, 3072], P(('dp', 'ctx'))
Inputs may be any that keep to these rules, and one draw needn't show every extreme that they name: `picture_starts`: piece r of a sequence starts between r * 256 and (r + 1) * 256 - 256, so pieces never intersect.
All inputs are finite; a program needn't handle non-finite values.
Results may differ from a plain program's by a relative error of at most 0.012.
The roundings to bfloat16 on the way count: a program that leaves them out, or rounds other values in their place, can miss the bound.
Values may be sent and summed in bfloat16 or wider, within the bound.
A program may use at most 256 MiB of HBM per device.

v0:
```python
import math

import jax
import jax.numpy as jnp
from jax import lax
from jax.sharding import PartitionSpec as P

H = 16
HD = 64
ROT = 16
PIC = 256
PICS = 4


norm_eps = 1e-05
clip_bound = 8.0
rotary_base = 10000.0
masked_score = -1e30


def exact_gelu(values):
    return jax.nn.gelu(values, approximate=False)


def rotate(values, positions, turn_sign):
    half_rot = ROT // 2
    inv_freq = rotary_base ** (-2.0 * jnp.arange(half_rot, dtype=jnp.float32) / ROT)
    angles = positions.astype(jnp.float32)[:, None] * inv_freq[None, :]
    cosine = jnp.cos(angles)[None, :, None, :]
    sine_part = turn_sign * jnp.sin(angles)[None, :, None, :]
    lead_half = values[..., :half_rot]
    tail_half = values[..., half_rot:ROT]
    return jnp.concatenate(
        [
            lead_half * cosine - tail_half * sine_part,
            tail_half * cosine + lead_half * sine_part,
            values[..., ROT:],
        ],
        axis=-1,
    )


def positions_of(row_numbers, group_order, group_len):
    group_ids = row_numbers // group_len
    owners = jnp.arange(group_order.shape[0], dtype=jnp.int32)
    placed = jnp.sum(
        jnp.where(group_ids[:, None] == owners[None, :], group_order[None, :], 0), axis=1
    )
    return placed * group_len + row_numbers % group_len


def piece_ids(positions, picture_starts):
    inside = (positions[None, None, :] >= picture_starts[:, :, None]) & (
        positions[None, None, :] < picture_starts[:, :, None] + PIC
    )
    labels = jnp.arange(1, PICS + 1, dtype=jnp.int32)[None, :, None]
    return jnp.sum(jnp.where(inside, labels, 0), axis=1)


def allowed_for(query_pos, query_ids, key_pos, key_ids):
    causal = key_pos[None, None, :] <= query_pos[None, :, None]
    same_piece = (query_ids[:, :, None] == key_ids[:, None, :]) & (query_ids[:, :, None] > 0)
    return (causal | same_piece)[:, None]


def blocked(running, pieces, group_len, step_fn):
    piece_len = pieces[0].shape[1]
    step_len = math.gcd(piece_len, group_len)

    def one_block(current, block_index):
        row_begin = block_index * step_len
        parts = tuple(
            (lax.dynamic_slice_in_dim(member, row_begin, step_len, 1) for member in pieces)
        )
        return (step_fn(current, parts, row_begin), None)

    running, _ = lax.scan(one_block, running, jnp.arange(piece_len // step_len, dtype=jnp.int32))
    return running


def shards(
    hidden_in,
    out_cotangent,
    attn_gain,
    attn_shift,
    qkv_weight,
    qkv_bias,
    proj_weight,
    proj_bias,
    mlp_gain,
    mlp_shift,
    up_weight,
    up_bias,
    down_weight,
    down_bias,
    picture_starts,
    group_order,
):
    batch_size, group_len, model_dim = hidden_in.shape
    token_rows = batch_size * group_len
    shard_rows = attn_gain.shape[0]
    ff_dim = up_weight.shape[1]
    ff_ratio = ff_dim // model_dim
    score_scale = HD ** (-0.5)
    f32 = jnp.float32
    bf16 = jnp.bfloat16
    hidden = hidden_in.reshape(token_rows, model_dim).astype(f32)
    centered = hidden - jnp.mean(hidden, axis=1, keepdims=True)
    inv_std = lax.rsqrt(jnp.mean(centered * centered, axis=1, keepdims=True) + norm_eps)
    normed = centered * inv_std
    own_rows = lax.axis_index("ctx") * group_len + jnp.arange(group_len, dtype=jnp.int32)
    own_pos = positions_of(own_rows, group_order, group_len)
    own_ids = piece_ids(own_pos, picture_starts)
    small_local = jnp.concatenate(
        [
            jnp.stack([attn_gain, attn_shift, mlp_gain, mlp_shift, proj_bias, down_bias], axis=1),
            qkv_bias.reshape(shard_rows, 3),
            up_bias.reshape(shard_rows, ff_ratio),
        ],
        axis=1,
    )
    down_rows = down_weight.reshape(shard_rows, ff_ratio * model_dim)
    small_piece = lax.all_gather(small_local, ("dp", "ctx"), axis=0, tiled=True)
    qkv_piece = lax.all_gather(qkv_weight, ("dp", "ctx"), axis=0, tiled=True)
    up_piece = lax.all_gather(up_weight, ("dp", "ctx"), axis=0, tiled=True)
    piece_len = qkv_piece.shape[0]
    small_f = small_piece.astype(f32)
    attn_piece = (normed * small_f[:, 0] + small_f[:, 1]).astype(bf16)
    mlp_piece = (normed * small_f[:, 2] + small_f[:, 3]).astype(bf16)
    qkv_sum = jnp.dot(attn_piece, qkv_piece, preferred_element_type=f32)
    up_sum = jnp.dot(mlp_piece, up_piece, preferred_element_type=f32)
    bias_table = small_f
    qkv_sum, up_sum, norm_attn, norm_mlp, bias_table = (
        qkv_sum,
        up_sum,
        attn_piece,
        mlp_piece,
        bias_table,
    )
    qkv_full = qkv_sum + bias_table[:, 6:9].reshape(-1)
    up_pre = up_sum + bias_table[:, 9:].reshape(-1)
    split_heads = qkv_full.reshape(batch_size, group_len, 3, H, HD)
    queries = rotate(split_heads[:, :, 0], own_pos, 1.0).astype(bf16)
    key_rows = rotate(split_heads[:, :, 1], own_pos, 1.0).astype(bf16)
    value_rows = split_heads[:, :, 2].astype(bf16)
    query_flat = queries.reshape(batch_size, group_len, model_dim)
    key_flat = key_rows.reshape(batch_size, group_len, model_dim)
    value_flat = value_rows.reshape(batch_size, group_len, model_dim)

    def forward_step(running, parts, row_begin):
        key_part, value_part = parts
        piece_len = key_part.shape[1]
        key_pos = positions_of(
            row_begin + jnp.arange(piece_len, dtype=jnp.int32), group_order, group_len
        )
        allowed = allowed_for(own_pos, own_ids, key_pos, piece_ids(key_pos, picture_starts))
        row_peak, row_total, summed = running
        key_heads = key_part.reshape(batch_size, piece_len, H, HD)
        value_heads = value_part.reshape(batch_size, piece_len, H, HD)
        scores = (
            jnp.einsum("bqhd,bkhd->bhqk", queries, key_heads, preferred_element_type=f32)
            * score_scale
        )
        masked = jnp.where(allowed, scores, masked_score)
        new_peak = jnp.maximum(row_peak, jnp.max(masked, axis=-1))
        row_fade = jnp.exp(row_peak - new_peak)
        weights = jnp.where(allowed, jnp.exp(masked - new_peak[..., None]), 0.0)
        row_total = row_total * row_fade + jnp.sum(weights, axis=-1)
        summed = summed * row_fade[..., None] + jnp.einsum(
            "bhqk,bkhd->bhqd", weights.astype(bf16), value_heads, preferred_element_type=f32
        )
        return (new_peak, row_total, summed)

    start_attn = (
        jnp.full((batch_size, H, group_len), masked_score, f32),
        jnp.zeros((batch_size, H, group_len), f32),
        jnp.zeros((batch_size, H, group_len, HD), f32),
    )
    row_peak, row_total, summed = blocked(
        start_attn,
        (
            lax.all_gather(key_flat, "ctx", axis=1, tiled=True),
            lax.all_gather(value_flat, "ctx", axis=1, tiled=True),
        ),
        group_len,
        forward_step,
    )
    log_total = row_peak + jnp.log(row_total)
    attended = (summed / row_total[..., None]).transpose(0, 2, 1, 3)
    attended_low = attended.reshape(token_rows, model_dim).astype(bf16)
    head_max = lax.pmax(jnp.max(row_peak, axis=(0, 2)), ("dp", "ctx"))
    act_low = exact_gelu(up_pre).astype(bf16)
    proj_piece = lax.all_gather(proj_weight, ("dp", "ctx"), axis=0, tiled=True)
    down_piece = lax.all_gather(down_rows, ("dp", "ctx"), axis=0, tiled=True)
    piece_len = proj_piece.shape[0]
    mix_sum = jnp.dot(attended_low, proj_piece, preferred_element_type=f32)
    mix_sum = mix_sum + jnp.dot(
        act_low, down_piece.reshape(piece_len * ff_ratio, model_dim), preferred_element_type=f32
    )
    block_out = (
        (hidden + mix_sum + bias_table[:, 4] + bias_table[:, 5])
        .astype(bf16)
        .reshape(batch_size, group_len, model_dim)
    )
    grad_y = out_cotangent.reshape(token_rows, model_dim)
    grad_yf = grad_y.astype(f32)
    proj_piece = lax.all_gather(proj_weight, ("dp", "ctx"), axis=0, tiled=True)
    down_piece = lax.all_gather(down_rows, ("dp", "ctx"), axis=0, tiled=True)
    piece_len = proj_piece.shape[0]
    attn_part = jnp.einsum("rd,nd->rn", grad_y, proj_piece, preferred_element_type=f32)
    act_part = jnp.einsum(
        "rd,md->rm",
        grad_y,
        down_piece.reshape(piece_len * ff_ratio, model_dim),
        preferred_element_type=f32,
    )
    grad_attn = attn_part
    grad_act = act_part
    grad_attn, grad_act = (grad_attn, grad_act)
    _, gelu_back = jax.vjp(exact_gelu, up_pre)
    grad_up = gelu_back(grad_act)[0].astype(bf16)
    grad_attended = grad_attn.astype(bf16)
    out_sum = jnp.sum(grad_yf, axis=0)
    out_width = model_dim + ff_ratio * model_dim + 1
    grad_heads = grad_attended.reshape(batch_size, group_len, H, HD)
    row_dot = jnp.sum(grad_heads.astype(f32) * attended, axis=-1).transpose(0, 2, 1)

    def query_step(running, parts, row_begin):
        key_part, value_part = parts
        piece_len = key_part.shape[1]
        key_pos = positions_of(
            row_begin + jnp.arange(piece_len, dtype=jnp.int32), group_order, group_len
        )
        allowed = allowed_for(own_pos, own_ids, key_pos, piece_ids(key_pos, picture_starts))
        key_heads = key_part.reshape(batch_size, piece_len, H, HD)
        value_heads = value_part.reshape(batch_size, piece_len, H, HD)
        scores = (
            jnp.einsum("bqhd,bkhd->bhqk", queries, key_heads, preferred_element_type=f32)
            * score_scale
        )
        masked = jnp.where(allowed, scores, masked_score)
        prob_rows = jnp.where(allowed, jnp.exp(masked - log_total[..., None]), 0.0)
        grad_prob = jnp.einsum(
            "bqhd,bkhd->bhqk", grad_heads, value_heads, preferred_element_type=f32
        )
        grad_scores = (prob_rows * (grad_prob - row_dot[..., None])).astype(bf16)
        return running + jnp.einsum(
            "bhqk,bkhd->bhqd", grad_scores, key_heads, preferred_element_type=f32
        )

    grad_query = (
        blocked(
            jnp.zeros((batch_size, H, group_len, HD), f32),
            (
                lax.all_gather(key_flat, "ctx", axis=1, tiled=True),
                lax.all_gather(value_flat, "ctx", axis=1, tiled=True),
            ),
            group_len,
            query_step,
        )
        * score_scale
    )
    log_total_all, row_dot_all = (
        lax.all_gather(log_total, "ctx", axis=2, tiled=True),
        lax.all_gather(row_dot, "ctx", axis=2, tiled=True),
    )

    def key_step(running, parts, row_begin):
        query_part, grad_part = parts
        piece_len = query_part.shape[1]
        query_pos = positions_of(
            row_begin + jnp.arange(piece_len, dtype=jnp.int32), group_order, group_len
        )
        allowed = allowed_for(query_pos, piece_ids(query_pos, picture_starts), own_pos, own_ids)
        total_part = lax.dynamic_slice_in_dim(log_total_all, row_begin, piece_len, 2)
        dot_part = lax.dynamic_slice_in_dim(row_dot_all, row_begin, piece_len, 2)
        grad_key, grad_value = running
        query_heads = query_part.reshape(batch_size, piece_len, H, HD)
        grad_piece = grad_part.reshape(batch_size, piece_len, H, HD)
        scores = (
            jnp.einsum("bqhd,bkhd->bhqk", query_heads, key_rows, preferred_element_type=f32)
            * score_scale
        )
        masked = jnp.where(allowed, scores, masked_score)
        prob_rows = jnp.where(allowed, jnp.exp(masked - total_part[..., None]), 0.0)
        grad_value = grad_value + jnp.einsum(
            "bhqk,bqhd->bhkd", prob_rows.astype(bf16), grad_piece, preferred_element_type=f32
        )
        grad_prob = jnp.einsum(
            "bqhd,bkhd->bhqk", grad_piece, value_rows, preferred_element_type=f32
        )
        grad_scores = (prob_rows * (grad_prob - dot_part[..., None])).astype(bf16)
        grad_key = grad_key + jnp.einsum(
            "bhqk,bqhd->bhkd", grad_scores, query_heads, preferred_element_type=f32
        )
        return (grad_key, grad_value)

    start_keys = (
        jnp.zeros((batch_size, H, group_len, HD), f32),
        jnp.zeros((batch_size, H, group_len, HD), f32),
    )
    grad_key, grad_value = blocked(
        start_keys,
        (
            lax.all_gather(query_flat, "ctx", axis=1, tiled=True),
            lax.all_gather(
                grad_attended.reshape(batch_size, group_len, model_dim), "ctx", axis=1, tiled=True
            ),
        ),
        group_len,
        key_step,
    )
    grad_key = grad_key * score_scale
    grad_q_back = rotate(grad_query.transpose(0, 2, 1, 3), own_pos, -1.0)
    grad_k_back = rotate(grad_key.transpose(0, 2, 1, 3), own_pos, -1.0)
    grad_v_back = grad_value.transpose(0, 2, 1, 3)
    grad_qkv = (
        jnp.stack([grad_q_back, grad_k_back, grad_v_back], axis=2)
        .reshape(token_rows, 3 * model_dim)
        .astype(bf16)
    )
    qkv_piece = lax.all_gather(qkv_weight, ("dp", "ctx"), axis=0, tiled=True)
    up_piece = lax.all_gather(up_weight, ("dp", "ctx"), axis=0, tiled=True)
    attn_part = jnp.einsum("re,ne->rn", grad_qkv, qkv_piece, preferred_element_type=f32)
    mlp_part = jnp.einsum("rf,nf->rn", grad_up, up_piece, preferred_element_type=f32)
    grad_norm_attn = attn_part
    grad_norm_mlp = mlp_part
    grad_norm_attn, grad_norm_mlp = (grad_norm_attn, grad_norm_mlp)
    gain_table = bias_table[:, 0:4]
    grad_norm = grad_norm_attn * gain_table[:, 0] + grad_norm_mlp * gain_table[:, 2]
    grad_hidden_f = grad_yf + inv_std * (
        grad_norm
        - jnp.mean(grad_norm, axis=1, keepdims=True)
        - normed * jnp.mean(grad_norm * normed, axis=1, keepdims=True)
    )
    grad_hidden = grad_hidden_f.astype(bf16).reshape(batch_size, group_len, model_dim)
    gain_grads = jnp.stack(
        [
            jnp.sum(grad_norm_attn * normed, axis=0),
            jnp.sum(grad_norm_attn, axis=0),
            jnp.sum(grad_norm_mlp * normed, axis=0),
            jnp.sum(grad_norm_mlp, axis=0),
        ],
        axis=1,
    )
    in_small = jnp.concatenate(
        [
            jnp.sum(grad_qkv.astype(f32), axis=0).reshape(model_dim, 3),
            jnp.sum(grad_up.astype(f32), axis=0).reshape(model_dim, ff_ratio),
            gain_grads,
        ],
        axis=1,
    )
    proj_part = jnp.einsum("rn,rd->nd", attended_low, grad_y, preferred_element_type=f32)
    down_part = jnp.einsum("rm,rd->md", act_low, grad_y, preferred_element_type=f32).reshape(
        model_dim, ff_ratio * model_dim
    )
    qkv_part = jnp.einsum("rn,re->ne", norm_attn, grad_qkv, preferred_element_type=f32)
    up_part = jnp.einsum("rn,rf->nf", norm_mlp, grad_up, preferred_element_type=f32)
    every_rows = lax.psum_scatter(
        jnp.concatenate(
            [
                jnp.concatenate([proj_part, down_part, out_sum[:, None]], axis=1),
                jnp.concatenate([qkv_part, up_part, in_small], axis=1),
            ],
            axis=1,
        ),
        ("dp", "ctx"),
        scatter_dimension=0,
        tiled=True,
    )
    out_rows = every_rows[:, :out_width]
    in_rows = every_rows[:, out_width:]
    grad_proj_weight = out_rows[:, :model_dim]
    grad_down_weight = out_rows[:, model_dim : model_dim + ff_ratio * model_dim].reshape(
        shard_rows * ff_ratio, model_dim
    )
    grad_bias_out = out_rows[:, out_width - 1]
    qkv_width = 3 * model_dim
    grad_qkv_weight = in_rows[:, :qkv_width]
    grad_up_weight = in_rows[:, qkv_width : qkv_width + ff_dim]
    tail_cols = in_rows[:, qkv_width + ff_dim :]
    grad_qkv_bias = tail_cols[:, :3].reshape(-1)
    grad_up_bias = tail_cols[:, 3 : 3 + ff_ratio].reshape(-1)
    gain_rows = tail_cols[:, 3 + ff_ratio :]
    clip_ratio = jnp.sqrt(clip_bound / jnp.maximum(head_max, clip_bound))
    head_cols = jnp.repeat(clip_ratio, HD)
    factor = jnp.concatenate([head_cols, head_cols, jnp.ones((model_dim,), f32)])
    clipped_qkv = qkv_weight.astype(f32) * factor[None, :]
    return (
        block_out,
        grad_hidden,
        gain_rows[:, 0],
        gain_rows[:, 1],
        grad_qkv_weight,
        grad_qkv_bias,
        grad_proj_weight,
        grad_bias_out,
        gain_rows[:, 2],
        gain_rows[:, 3],
        grad_up_weight,
        grad_up_bias,
        grad_down_weight,
        grad_bias_out,
        clipped_qkv,
    )


def solution(mesh):
    in_specs = (
        P("dp", "ctx", None),
        P("dp", "ctx", None),
        P(("dp", "ctx")),
        P(("dp", "ctx")),
        P(("dp", "ctx"), None),
        P(("dp", "ctx")),
        P(("dp", "ctx"), None),
        P(("dp", "ctx")),
        P(("dp", "ctx")),
        P(("dp", "ctx")),
        P(("dp", "ctx"), None),
        P(("dp", "ctx")),
        P(("dp", "ctx"), None),
        P(("dp", "ctx")),
        P("dp", None),
        P(),
    )
    out_specs = (
        P("dp", "ctx", None),
        P("dp", "ctx", None),
        P(("dp", "ctx")),
        P(("dp", "ctx")),
        P(("dp", "ctx"), None),
        P(("dp", "ctx")),
        P(("dp", "ctx"), None),
        P(("dp", "ctx")),
        P(("dp", "ctx")),
        P(("dp", "ctx")),
        P(("dp", "ctx"), None),
        P(("dp", "ctx")),
        P(("dp", "ctx"), None),
        P(("dp", "ctx")),
        P(("dp", "ctx"), None),
    )
    return jax.shard_map(shards, mesh=mesh, in_specs=in_specs, out_specs=out_specs, check_vma=False)
```

profile of v0, /device:TPU:0, one launch (start us, length us, event | category | flops | bytes accessed | tf_op | source)
XLA Modules:
  0.0 1450.7 jit_solution(7988186798000880355)
XLA Ops:
  17.4 43.8 %all-gather = bf16[32,32,13]{1,2,0:T(8,128)(2,1)S(1)} all-gather(bf16[1,32,13]{1,2,0:T(8,128)(2,1)S(1)} %copy.235), channel_id=1, replica_groups=mesh['dp'=2,'ctx'=16] {'dp','ctx'}, dimensions={0}, use_global_device_ids=true | all-gather | bytes 27456 | tf_op jit(solution)/shard_map/all_gather | solution.py:123
  65.3 18.1 %all-gather.10.cloned.1.call-done = bf16[1024,3072]{1,0:T(8,128)(2,1)} async-done(((bf16[32,3072]{1,0:T(8,128)(2,1)}), bf16[1024,3072]{1,0:T(8,128)(2,1)}) %all-gather.10.cloned.1.call-update) | async-done | bytes 6291472 | tf_op jit(solution)/shard_map/all_gather | solution.py:124
  83.4 3.8 convolution_add_fusion.5
  101.3 39.9 %all-gather.16.cloned.1.call-done = bf16[1024,1024]{1,0:T(8,128)(2,1)} async-done(((bf16[32,1024]{1,0:T(8,128)(2,1)}), bf16[1024,1024]{1,0:T(8,128)(2,1)}) %all-gather.16.cloned.1.call-update) | async-done | bytes 2097168 | tf_op jit(solution)/shard_map/all_gather | solution.py:193
  141.2 3.1 convolution_convert_fusion
  154.2 66.8 %all-gather.20.cloned.1.call-done = bf16[1024,4096]{1,0:T(8,128)(2,1)} async-done(((bf16[32,4096]{1,0:T(8,128)(2,1)}), bf16[1024,4096]{1,0:T(8,128)(2,1)}) %all-gather.20.cloned.1.call-update) | async-done | bytes 8388624 | tf_op jit(solution)/shard_map/all_gather | solution.py:194
  221.0 14.0 reshape.635
  235.0 64.8 %all-gather.18.cloned.1.call-done = bf16[1024,4096]{1,0:T(8,128)(2,1)} async-done(((bf16[32,4096]{1,0:T(8,128)(2,1)}), bf16[1024,4096]{1,0:T(8,128)(2,1)}) %all-gather.18.cloned.1.call-update) | async-done | bytes 8388624 | tf_op jit(solution)/shard_map/all_gather | solution.py:125
  299.8 4.8 convolution_add_fusion.4
  305.6 8.0 convert_reduce_fusion.1
  314.9 8.1 fusion.67
  323.1 20.4 %reshape.641 = f32[1024,4096]{1,0:T(8,128)} reshape(f32[4096,1024]{1,0:T(8,128)} %fusion.67) | data formatting | bytes 33554432 | tf_op jit(solution)/shard_map/reshape | solution.py:355
  343.4 8.2 fusion.69
  353.0 50.3 %all-gather.14.cloned.1.call-done = bf16[2,1024,1024]{2,1,0:T(8,128)(2,1)} async-done(((bf16[2,64,1024]{2,1,0:T(8,128)(2,1)}), bf16[2,1024,1024]{2,1,0:T(8,128)(2,1)}) %all-gather.14.cloned.1.call-update) | async-done | bytes 4194320 | tf_op jit(solution)/shard_map/all_gather | solution.py:183
  403.3 78.1 %while.45 = (s32[]{:T(128)}, f32[2,16,64]{2,1,0:T(8,128)S(1)}, f32[2,16,64]{2,1,0:T(8,128)S(1)}, f32[2,16,64,64]{3,2,1,0:T(8,128)S(1)}, s32[16]{0:T(128)S(1)}, /...) while((s32[]{:T(128)}, f32[2,16,64]{2,1,0:T(8,128)S(1)}, ...), condition=%wide.region_9.10_spmd.clone, body=%wide.region_4.9_spmd.clone.sunk | while | flops 35173712 | bytes 5681871 | solution.py:77
  484.1 27.7 %all_gather.47 = f32[2,16,1024]{1,0,2:T(2,128)S(1)} all-gather(f32[2,16,64]{1,0,2:T(2,128)S(1)} %add.499), channel_id=1, replica_groups=mesh['dp'=2,'ctx'=16] {'ctx'}, dimensions={2}, use_global_device_ids=true | all-gather | bytes 139264 | tf_op jit(solution)/shard_map/all_gather | solution.py:264
  513.6 21.4 %all_gather.49 = f32[2,16,1024]{1,0,2:T(2,128)S(1)} all-gather(f32[2,16,64]{1,0,2:T(2,128)S(1)} %copy.256), channel_id=1, replica_groups=mesh['dp'=2,'ctx'=16] {'ctx'}, dimensions={2}, use_global_device_ids=true | all-gather | bytes 139264 | tf_op jit(solution)/shard_map/all_gather | solution.py:265
  535.5 163.1 %while.47 = (s32[]{:T(128)}, f32[2,16,64,64]{3,2,1,0:T(8,128)S(1)}, f32[2,16,64,64]{3,2,1,0:T(8,128)}, s32[64]{0:T(128)S(1)}, s32[16]{0:T(128)S(1)}, /*index=5*/...) while((s32[]{:T(128)}, f32[2,16,64,64]{3,2,1,0:T(8,128)S(1)}, ...), condition=%wide.region_18.19_spmd.clone, body=%wide.region_15.18_spmd.clone.sunk | while | flops 68717904 | bytes 8468362 | solution.py:77
  552.1 2.6 convolution_add_fusion.14
  562.4 2.6 convolution_add_fusion.14
  572.7 2.6 convolution_add_fusion.14
  583.0 2.6 convolution_add_fusion.14
  593.2 2.6 convolution_add_fusion.14
  700.7 107.1 %while.46 = (s32[]{:T(128)}, f32[2,16,64,64]{3,2,1,0:T(8,128)S(1)}, s32[16]{0:T(128)S(1)}, s32[16]{0:T(128)S(1)}, s32[64]{0:T(128)S(1)}, /*index=5*/s32[2,64]{1,...) while((s32[]{:T(128)}, f32[2,16,64,64]{3,2,1,0:T(8,128)S(1)}, ...), condition=%wide.region_14.15_spmd.clone, body=%wide.region_11.14_spmd.clone.sunk | while | flops 51547472 | bytes 5550805 | solution.py:77
  814.3 2.8 fusion.66
  818.4 7.5 fusion.68
  828.1 7.2 fusion.54
  837.8 62.2 %concatenate.26 = f32[1024,12300]{1,0:T(8,128)} concatenate(f32[1024,1024]{1,0:T(8,128)} %fusion.66, f32[1024,4096]{1,0:T(8,128)} %reshape.641, f32[1024,1]{1,0:T(8,128)S(1)} %copy-done.22, f32[1024,3072]{1,0:T(8,128)} %fusion.68, f32[1024,4096]{1,0:T(8,128)} %fusion.69, f32[1024,3]{1,0:T(8,128)S(1)} %copy-done.24, f32[1024,4]{1,0:T(8,128)S(1)} %copy-done.23, ...), dimensions={1} | concatenate | bytes 100761600 | tf_op jit(solution)/shard_map/concatenate | solution.py:361
  901.3 4.7 fusion.64
  906.0 61.8 %pmax.7 = f32[16]{0:T(128)S(1)} all-reduce(f32[16]{0:T(128)S(1)} %reduce_max.21), channel_id=1, replica_groups=mesh['dp'=2,'ctx'=16] {'dp','ctx'}, use_global_device_ids=true, to_apply=%region_30.31 | all-reduce | flops 16 | bytes 128 | tf_op jit(solution)/shard_map/pmax | solution.py:191
  969.0 2.8 fusion.50
  972.6 459.6 %reduce-scatter.2.cloned.1.call-done = f32[32,12300]{1,0:T(8,128)} async-done(((f32[1024,12300]{1,0:T(8,128)}), f32[32,12300]{1,0:T(8,128)}) %reduce-scatter.2.cloned.1.call-update) | async-done | bytes 1574416 | tf_op jit(solution)/shard_map/reduce_scatter | solution.py:360
  (1246 shorter events, 373.7 us)
Async XLA Ops:
  7.2 54.3 %copy-start.9 = (bf16[2,64,1024]{2,1,0:T(8,128)(2,1)S(1)}, bf16[2,64,1024]{2,1,0:T(8,128)(2,1)}, u32[]{:S(2)}) copy-start(bf16[2,64,1024]{2,1,0:T(8,128)(2,1)} %param.22) | copy-start | bytes 786436
  7.2 55.5 %copy-start.48 = (s32[16]{0:T(128)S(1)}, s32[16]{0:T(128)}, u32[]{:S(2)}) copy-start(s32[16]{0:T(128)} %param.37) | copy-start | bytes 196
  7.2 76.2 %all-gather.10.cloned.1.call-start = ((), (), s32[]{:S(2)}) async-start(), calls=%async_computation.1 | async-start | bytes 6488064 | tf_op jit(solution)/shard_map/all_gather | solution.py:124
  7.9 133.3 %all-gather.16.cloned.1.call-start = ((), (), s32[]{:S(2)}) async-start(), calls=%async_computation.4 | async-start | bytes 2162688 | tf_op jit(solution)/shard_map/all_gather | solution.py:193
  8.7 212.3 %all-gather.20.cloned.1.call-start = ((), (), s32[]{:S(2)}) async-start(), calls=%async_computation.6 | async-start | bytes 8650752 | tf_op jit(solution)/shard_map/all_gather | solution.py:194
  10.6 289.2 %all-gather.18.cloned.1.call-start = ((), (), s32[]{:S(2)}) async-start(), calls=%async_computation.5 | async-start | bytes 8650752 | tf_op jit(solution)/shard_map/all_gather | solution.py:125
  11.2 341.8 %all-gather.12.cloned.1.call-start = ((), (), s32[]{:S(2)}) async-start(), calls=%async_computation.2 | async-start | bytes 4456448 | tf_op jit(solution)/shard_map/all_gather | solution.py:182
  61.7 25.5 %copy-start.42 = (f32[128]{0:T(128)}, f32[128]{0:T(128)S(1)}, u32[]{:S(2)}) copy-start(f32[128]{0:T(128)S(1)} %div.80) | copy-start | bytes 1540
  61.9 25.3 %copy-start.46 = (f32[2,64]{1,0:T(2,128)}, f32[2,64]{1,0:T(2,128)S(1)}, u32[]{:S(2)}) copy-start(f32[2,64]{1,0:T(2,128)S(1)} %add_rsqrt_fusion) | copy-start | bytes 1540
  62.0 25.2 %copy-start.44 = (f32[128]{0:T(128)}, f32[128]{0:T(128)S(1)}, u32[]{:S(2)}) copy-start(f32[128]{0:T(128)S(1)} %rsqrt.13) | copy-start | bytes 1540
  64.3 22.9 %copy-start.34 = (f32[1024,1]{0,1:T(1,128)}, f32[1024,1]{0,1:T(1,128)S(1)}, u32[]{:S(2)}) copy-start(f32[1024,1]{0,1:T(1,128)S(1)} %get-tuple-element.909) | copy-start | bytes 12292
  64.3 22.9 %copy-start.36 = (f32[1024,1]{0,1:T(1,128)}, f32[1024,1]{0,1:T(1,128)S(1)}, u32[]{:S(2)}) copy-start(f32[1024,1]{0,1:T(1,128)S(1)} %get-tuple-element.910) | copy-start | bytes 12292
  97.4 43.8 %copy-start.11 = (bf16[2,64,1024]{2,1,0:T(8,128)(2,1)S(1)}, bf16[2,64,1024]{2,1,0:T(8,128)(2,1)}, u32[]{:S(2)}) copy-start(bf16[2,64,1024]{2,1,0:T(8,128)(2,1)} %param.23) | copy-start | bytes 786436
  97.4 305.9 %all-gather.14.cloned.1.call-start = ((), (), s32[]{:S(2)}) async-start(), calls=%async_computation.3 | async-start | bytes 4456448 | tf_op jit(solution)/shard_map/all_gather | solution.py:183
  101.2 43.8 %copy-start.40 = (f32[64,8]{0,1:T(8,128)S(1)}, f32[64,8]{0,1:T(8,128)}, u32[]{:S(2)}) copy-start(f32[64,8]{0,1:T(8,128)} %get-tuple-element.914) | copy-start | bytes 6148
  101.2 434.2 %all-gather.24.cloned.1.call-start = ((), (), s32[]{:S(2)}) async-start(), calls=%async_computation.8 | async-start | bytes 4456448 | tf_op jit(solution)/shard_map/all_gather | solution.py:306
  144.4 391.1 %all-gather.22.cloned.1.call-start = ((), (), s32[]{:S(2)}) async-start(), calls=%async_computation.7 | async-start | bytes 4456448 | tf_op jit(solution)/shard_map/all_gather | solution.py:305
  154.0 145.8 %copy-start.18 = (bf16[128,1024]{1,0:T(8,128)(2,1)S(1)}, bf16[128,1024]{1,0:T(8,128)(2,1)}, u32[]{:S(2)}) copy-start(bf16[128,1024]{1,0:T(8,128)(2,1)} %get-tuple-element.903) | copy-start | bytes 786436
  154.0 1278.1 %reduce-scatter.2.cloned.1.call-start = ((), (), s32[]{:S(2)}) async-start(), calls=%async_computation.9 | async-start | bytes 52445184 | tf_op jit(solution)/shard_map/reduce_scatter | solution.py:360
  299.8 5.8 copy-start
  313.6 29.9 %copy-start.16 = (bf16[128,4096]{1,0:T(8,128)(2,1)}, bf16[128,4096]{1,0:T(8,128)(2,1)S(1)}, u32[]{:S(2)}) copy-start(bf16[128,4096]{1,0:T(8,128)(2,1)S(1)} %get-tuple-element.868) | copy-start | bytes 3145732
  343.4 59.9 %copy-start.49 = (s32[16]{0:T(128)S(1)}, s32[16]{0:T(128)}, u32[]{:S(2)}) copy-start(s32[16]{0:T(128)} %param.37) | copy-start | bytes 196
  481.4 30.4 %copy-start.4 = (bf16[2,64,16,64]{3,1,2,0:T(8,128)(2,1)}, bf16[2,64,16,64]{3,1,2,0:T(8,128)(2,1)S(1)}, u32[]{:S(2)}) copy-start(bf16[2,64,16,64]{3,1,2,0:T(8,128)(2,1)S(1)} %get-tuple-element.1376) | copy-start | bytes 786436
  481.8 31.1 %copy-start.14 = (bf16[2,64,16,64]{3,2,1,0:T(8,128)(2,1)S(1)}, bf16[2,64,16,64]{3,2,1,0:T(8,128)(2,1)}, u32[]{:S(2)}) copy-start(bf16[2,64,16,64]{3,2,1,0:T(8,128)(2,1)} %copy-done.13) | copy-start | bytes 786436
  512.9 22.6 %copy-start.50 = (s32[16]{0:T(128)S(1)}, s32[16]{0:T(128)}, u32[]{:S(2)}) copy-start(s32[16]{0:T(128)} %param.37) | copy-start | bytes 196
  513.5 22.0 %copy-start.2 = (f32[2,16,64,64]{3,2,1,0:T(8,128)S(1)}, f32[2,16,64,64]{3,2,1,0:T(8,128)}, u32[]{:S(2)}) copy-start(f32[2,16,64,64]{3,2,1,0:T(8,128)} %custom-call.4) | copy-start | bytes 1572868
  814.3 11.5 slice-start
  818.3 7.5 slice-start.1
  901.3 66.7 %copy-start.25 = (f32[128,1024]{1,0:T(8,128)S(1)}, f32[128,1024]{1,0:T(8,128)}, u32[]{:S(2)}) copy-start(f32[128,1024]{1,0:T(8,128)} %get-tuple-element.899) | copy-start | bytes 1572868
  901.3 67.7 %copy-start.21 = (bf16[128,1024]{1,0:T(8,128)(2,1)S(1)}, bf16[128,1024]{1,0:T(8,128)(2,1)}, u32[]{:S(2)}) copy-start(bf16[128,1024]{1,0:T(8,128)(2,1)} %convert_element_type.150) | copy-start | bytes 786436
  901.3 67.7 %copy-start.37 = (f32[1024,1]{0,1:T(1,128)S(1)}, f32[1024,1]{0,1:T(1,128)}, u32[]{:S(2)}) copy-start(f32[1024,1]{0,1:T(1,128)} %get-tuple-element.906) | copy-start | bytes 12292
  901.3 67.7 %copy-start.38 = (f32[1024,1]{0,1:T(1,128)S(1)}, f32[1024,1]{0,1:T(1,128)}, u32[]{:S(2)}) copy-start(f32[1024,1]{0,1:T(1,128)} %get-tuple-element.907) | copy-start | bytes 12292
  (124 other events, 295.8 us)
Sparse Core Ops, SparseCore 0:
  10.9 72.4 all-gather.9
  86.2 54.9 all-gather.15
  144.6 76.3 all-gather.19
  223.7 76.0 all-gather.17
  302.4 49.1 all-gather.11
  354.2 49.0 all-gather.13
  405.5 49.0 all-gather.23
  457.4 56.9 all-gather.21
  900.2 531.9 reduce-scatter.1
where the time goes:
time: 1470 us; the launch traced here: 1450 us
  waiting for transfers between devices  702 us (48%)
  local copies, waits for them, and re-layouts  280 us (19%)
  matrix products  225 us (15%)
  blocking collectives  155 us (11%)
  loops' own time  37.1 us (3%)
  other arithmetic  36.1 us (2%)
  between operations  15.1 us (1%)
    reduce_scatter x1, waiting for transfers between devices, shards(): lax.psum_scatter(jnp.concatenate([jnp.concatenate([proj_part, down_part,...  460 us
    all_gather x1, waiting for transfers between devices, shards(): down_piece = lax.all_gather(down_rows, ('dp', 'ctx'), axis=0, tiled=True)  66.8 us
    all_gather x1, waiting for transfers between devices, shards(): up_piece = lax.all_gather(up_weight, ('dp', 'ctx'), axis=0, tiled=True)  64.8 us
    concatenate x1, local copies, waits for them, and re-layouts, shards(): jnp.concatenate([jnp.concatenate([proj_part, down_part, out_sum[:, None]]...  62.2 us
    pmax x1, blocking collectives, shards(): head_max = lax.pmax(jnp.max(row_peak, axis=(0, 2)), ('dp', 'ctx'))  61.8 us
    dynamic_slice x48, local copies, waits for them, and re-layouts, one_block(): lax.dynamic_slice_in_dim(member, row_begin, step_len, 1)  51.7 us
    all_gather x1, waiting for transfers between devices, shards(): lax.all_gather(value_flat, 'ctx', axis=1, tiled=True)  50.3 us
    all_gather x1, blocking collectives, shards(): small_piece = lax.all_gather(small_local, ('dp', 'ctx'), axis=0, tiled=True)  43.8 us
  transfers between devices with their start and end apart: 9, of which 6 were waited for; matrix products, arithmetic and copies ran while one was open for 13% of the time, Pallas kernels for 0%

commit v1 on v0

--- a/solution.py
+++ b/solution.py
@@ -3,6 +3,8 @@
 import jax
 import jax.numpy as jnp
 from jax import lax
+from jax.experimental import pallas as pl
+from jax.experimental.pallas import tpu as pltpu
 from jax.sharding import PartitionSpec as P
 
 H = 16
@@ -406,6 +408,705 @@
     )
 
 
+MESH = pl.DeviceIdType.MESH
+NT = (((1,), (1,)), ((), ()))
+f32 = jnp.float32
+bf16 = jnp.bfloat16
+CH = 8
+NC = 16
+SL = 1024
+TOK = 2048
+D = 1024
+
+
+def dot(a, b):
+    return jnp.dot(a, b, preferred_element_type=f32)
+
+
+def dot_nt(a, b):
+    return lax.dot_general(a, b, NT, preferred_element_type=f32)
+
+
+def block_kernel(
+    go_ref, ps_ref, x_ref, dy_ref, ws_ref, pw_ref, dw_ref,
+    bo_ref, gh_ref, gr_ref, gp_ref, sr_ref, ds_ref,
+    X, Y, NA, NM, WC, WPD, CT, ST, PK, LIM, SM, BV,
+    Q, K, V, VT, KT, PT, ATT, AA, GP, DA, GG, DQ, DK, DV, HM, GN,
+    TT, G, GY, GS, PDS, PDR, SROW, DSUM,
+    TMP, LP, SB, RSB, SR, RR,
+    w_s, w_r, wy_s, wy_r, pd_s, pd_r, ga_s, ga_r, rs_s, rs_r,
+    gy_s, gy_r, gg_s, gg_r, gpd_s, gpd_r, sm_s, sm_r, dm_s, dm_r,
+):
+    d = lax.axis_index("dp")
+    c = lax.axis_index("ctx")
+    k = c // 2
+    j = c % 2
+    z = k // 2
+    r = z + (k % 2) * (7 - 2 * z)
+    head = 8 * j + k
+
+    def ctx_of(pos, core):
+        p = (pos + 16) % 8
+        return 2 * (2 * p + (p // 4) * (15 - 4 * p)) + core
+
+    right = (d, ctx_of(r + 1, j))
+    left = (d, ctx_of(r - 1, j))
+    sibling = (d, 2 * k + (1 - j))
+    partner = (1 - d, c)
+
+    def rcopy(src, dst, ss, rs, dev):
+        return pltpu.make_async_remote_copy(
+            src_ref=src, dst_ref=dst, send_sem=ss, recv_sem=rs,
+            device_id=dev, device_id_type=MESH,
+        )
+
+    barrier = pltpu.get_barrier_semaphore()
+
+    def hello(o, _):
+        lin = (d * NC + c + o) % 32
+        pl.semaphore_signal(barrier, inc=1, device_id=(lin // NC, lin % NC), device_id_type=MESH)
+        return 0
+
+    lax.fori_loop(1, 32, hello, 0)
+    pl.semaphore_wait(barrier, 31)
+
+    def w_copy(o, dst_c, row):
+        return rcopy(
+            ws_ref.at[8 * (dst_c % 2) + dst_c // 2],
+            WC.at[pl.ds(pl.multiple_of(row, 32), 32)],
+            w_s.at[o], w_r.at[o], (d, dst_c),
+        )
+
+    own_row = 32 * (NC * d + c)
+
+    def w_send(o, _):
+        w_copy(o, (c + o) % NC, own_row).start()
+        return 0
+
+    lax.fori_loop(1, NC, w_send, 0)
+
+    class Gather:
+        def __init__(self, buf, own, s, i):
+            self.buf, self.own, self.s, self.i = buf, own, s, i
+
+        def at(self, delta, core, lo=0, n=64):
+            row = self.s * SL + 64 * ctx_of(r + delta, core) + lo
+            return self.buf.at[pl.ds(pl.multiple_of(row, 32), n)]
+
+        def ring(self, t, way):
+            delta = -t if way == 0 else t
+            region = self.at(delta, j) if t < 3 else self.at(delta, j, 32 * way, 32)
+            slot = 4 * way + t
+            return rcopy(region, region, ga_s.at[self.i, slot], ga_r.at[self.i, slot],
+                         right if way == 0 else left)
+
+        def arrival(self, t, way):
+            delta = -(t + 1) if way == 0 else t + 1
+            region = self.at(delta, j) if t < 3 else self.at(delta, j, 32 * way, 32)
+            slot = 4 * way + t
+            return rcopy(region, region, ga_s.at[self.i, slot], ga_r.at[self.i, slot],
+                         right if way == 0 else left)
+
+        def sib(self, slot, core):
+            delta = (0, -1, -2, -3, 1, 2, 3, 4)[slot]
+            region = self.at(delta, core)
+            return rcopy(region, region, ga_s.at[self.i, 8 + slot], ga_r.at[self.i, 8 + slot], sibling)
+
+        def start(self):
+            row = self.s * SL + 64 * c
+            self.buf[pl.ds(pl.multiple_of(row, 64), 64), :] = self.own[self.s * 64:self.s * 64 + 64, :]
+            self.ring(0, 0).start()
+            self.ring(0, 1).start()
+            self.sib(0, j).start()
+
+        def pump(self, t):
+            for way in (0, 1):
+                self.arrival(t - 1, way).wait_recv()
+                if t < 4:
+                    self.ring(t, way).start()
+                    self.sib((t if way == 0 else 3 + t), j).start()
+            if t == 4:
+                self.sib(7, j).start()
+
+        def finish(self):
+            for slot in range(8):
+                self.sib(slot, 1 - j).wait_recv()
+
+        def drain(self):
+            for t in range(4):
+                self.ring(t, 0).wait_send()
+                self.ring(t, 1).wait_send()
+            for slot in range(8):
+                self.sib(slot, j).wait_send()
+
+    gx = [Gather(X, x_ref, s, s) for s in range(2)]
+    gd = [Gather(Y, dy_ref, s, 2 + s) for s in range(2)]
+    gx[0].start()
+    gx[1].start()
+
+    def pd_copies(jj, dst_dp):
+        dev = (dst_dp, 2 * k + d)
+        return (
+            rcopy(pw_ref, WPD.at[pl.ds(256 + 32 * jj, 32)], pd_s.at[dst_dp, 0], pd_r.at[jj, 0], dev),
+            rcopy(dw_ref, WPD.at[pl.ds(128 * jj, 128)], pd_s.at[dst_dp, 1], pd_r.at[jj, 1], dev),
+        )
+
+    here = d == j
+    for e in range(2):
+        @pl.when(jnp.logical_not(here & (d == e)))
+        def _():
+            for cp in pd_copies(j, e):
+                cp.start()
+
+    @pl.when(here)
+    def _():
+        WPD[pl.ds(256 + 32 * j, 32), :] = pw_ref[...]
+        WPD[pl.ds(128 * j, 128), :] = dw_ref[...]
+    WPD[320:384, :] = jnp.zeros((64, D), bf16)
+
+    WC[pl.ds(pl.multiple_of(own_row, 32), 32), :] = ws_ref[head]
+
+    def lane(shape):
+        return lax.broadcasted_iota(jnp.int32, shape, len(shape) - 1)
+
+    rows_i = lax.broadcasted_iota(jnp.int32, (SL, 128), 0)
+    place = jnp.zeros((SL, 128), jnp.int32)
+    cols_i = lane((8, SL))
+    place_row = jnp.zeros((8, SL), jnp.int32)
+    for b in range(NC):
+        gob = go_ref[b]
+        place = jnp.where((rows_i >> 6) == b, gob, place)
+        place_row = jnp.where((cols_i >> 6) == b, gob, place_row)
+    place = place * 64 + (rows_i & 63)
+    place_row = place_row * 64 + (cols_i & 63)
+    PK[...] = place
+    for s in range(2):
+        lim = place_row
+        for p in range(PICS):
+            st = ps_ref[s, p]
+            lim = jnp.where((place_row >= st) & (place_row < st + PIC), st + (PIC - 1), lim)
+        LIM[s] = lim
+
+    def make_table(i, _):
+        rows = pl.ds(pl.multiple_of(i * 128, 128), 128)
+        ln = lane((128, 128))
+        l64 = ln & 63
+        freq = jnp.zeros((128, 128), f32)
+        for q in range(ROT // 2):
+            freq = jnp.where((l64 & 7) == q, float(rotary_base ** (-2.0 * q / ROT)), freq)
+        ang = PK[rows, :].astype(f32) * freq
+        CT[rows, :] = jnp.where(l64 < ROT, jnp.cos(ang), 1.0)
+        sn = jnp.sin(ang)
+        ST[rows, :] = jnp.where(l64 < ROT // 2, -sn, jnp.where(l64 < ROT, sn, 0.0))
+        return 0
+
+    lax.fori_loop(0, SL // 128, make_table, 0)
+
+    half = pl.ds(pl.multiple_of(512 * d, 512), 512)
+    other = pl.ds(pl.multiple_of(512 * (1 - d), 512), 512)
+
+    def w_wait(o, _):
+        src_c = (c - o + NC) % NC
+        w_copy(o, (c + o) % NC, 32 * (NC * d + src_c)).wait_recv()
+        return 0
+
+    lax.fori_loop(1, NC, w_wait, 0)
+    wy = rcopy(WC.at[half], WC.at[half], wy_s, wy_r, partner)
+    wy.start()
+    for t in range(1, 5):
+        gx[0].pump(t)
+        gx[1].pump(t)
+    gd[0].start()
+    gd[1].start()
+    rcopy(WC.at[other], WC.at[other], wy_s, wy_r, partner).wait_recv()
+
+    for jj in range(2):
+        @pl.when(jnp.logical_not(here & (j == jj)))
+        def _():
+            for cp in pd_copies(jj, 0):
+                cp.wait_recv()
+
+    SM[...] = WC[:, 128:256].astype(f32).T[64:80, :]
+    en = lane((16, 256))
+    vrow = lax.broadcasted_iota(jnp.int32, (16, 256), 0)
+    feat = lax.broadcasted_iota(jnp.int32, (D, 256), 0)
+    jl = lane((D, 256))
+    smb = SM[...].astype(bf16)
+
+    def pick(e_big, e_small, div, first):
+        n_big = div(e_big)
+        onehot = jnp.where(feat == n_big, 1.0, 0.0).astype(bf16)
+        got = dot(smb, onehot)
+        width = 3 if first == 6 else 4
+        return jnp.sum(jnp.where(vrow == first + e_small - width * div(e_small), got, 0.0), axis=0, keepdims=True)
+
+    def e_qkv(ln):
+        return SL * (ln >> 6) + HD * head + (ln & 63)
+
+    bq = pick(e_qkv(jl), e_qkv(en), lambda e: (e * 43691) >> 17, 6)
+    bq = jnp.where(lane((1, 256)) < 192, bq, 0.0)
+    bu = pick(256 * head + jl, 256 * head + en, lambda e: e >> 2, 9)
+    BV[0] = jnp.broadcast_to(bq, (8, 256))
+    BV[1] = jnp.broadcast_to(bu, (8, 256))
+
+    ln128 = lane((128, 128))
+    low_half = ln128 < 64
+
+    def turn(v, cs, sn, sign):
+        l64 = lane(v.shape) & 63
+        mate = jnp.where(l64 < ROT // 2, pltpu.roll(v, 120, 1), pltpu.roll(v, 8, 1))
+        return v * cs + sign * (mate * sn)
+
+    def normed_of(rows_value):
+        x = rows_value.astype(f32)
+        cen = x - jnp.mean(x, axis=1, keepdims=True)
+        inv = lax.rsqrt(jnp.mean(cen * cen, axis=1, keepdims=True) + norm_eps)
+        return cen * inv, inv
+
+    def n_stage(i, _):
+        rows = pl.ds(pl.multiple_of(i * 128, 128), 128)
+        trow = pl.ds(pl.multiple_of((i % 8) * 128, 128), 128)
+        nrm, _ = normed_of(X[rows, :])
+        na = (nrm * SM[0:1, :] + SM[1:2, :]).astype(bf16)
+        nm = (nrm * SM[2:3, :] + SM[3:4, :]).astype(bf16)
+        NA[rows, :] = na
+        NM[rows, :] = nm
+        qkv = dot(na, WC[:, 0:256]) + BV[0, 0:1, :]
+        up = dot(nm, WC[:, 256:512]) + BV[1, 0:1, :]
+        rot = turn(qkv[:, 0:128], CT[trow, :], ST[trow, :], 1.0)
+        Q[rows, :] = jnp.where(low_half, rot * 0.125, 0.0).astype(bf16)
+        K[rows, :] = jnp.where(low_half, pltpu.roll(rot, 64, 1), 0.0).astype(bf16)
+        V[rows, :] = jnp.where(low_half, qkv[:, 128:256], 0.0).astype(bf16)
+        cdf = 0.5 * (1.0 + lax.erf(up * (2.0 ** -0.5)))
+        AA[rows, 0:256] = (up * cdf).astype(bf16)
+        GP[rows, :] = cdf + up * (jnp.exp(-0.5 * up * up) * ((2.0 * math.pi) ** -0.5))
+        return 0
+
+    for s in range(2):
+        gx[s].finish()
+        lax.fori_loop(8 * s, 8 * s + 8, n_stage, 0)
+        for t in range(1, 3):
+            gd[s].pump(t)
+
+    for s in range(2):
+        VT[s] = V[s * SL:s * SL + SL, :].astype(f32).T.astype(bf16)
+        KT[s] = K[s * SL:s * SL + SL, :].astype(f32).T.astype(bf16)
+
+    HM[...] = jnp.full((8, 256), masked_score, f32)
+
+    def fwd(i, _):
+        s = i // 4
+        q0 = pl.multiple_of((i % 4) * 256, 256)
+        rows = pl.ds(pl.multiple_of(i * 256, 256), 256)
+        seq = pl.ds(pl.multiple_of(s * SL, SL), SL)
+        st = dot_nt(K[seq, :], Q[rows, :])
+        pk = PK[...]
+        lim = LIM[s, 0:1, pl.ds(q0, 256)]
+        masked = jnp.where(jnp.concatenate([pk, pk], axis=1) <= lim, st, masked_score)
+        peak = jnp.max(masked, axis=0, keepdims=True)
+        p = jnp.exp(masked - peak)
+        tot = jnp.sum(p, axis=0, keepdims=True)
+        pt = (p * (1.0 / tot)).astype(bf16)
+        PT[i] = pt
+        at = dot(VT[s], pt)
+        ATT[i] = at
+        AA[rows, 256:384] = at.T.astype(bf16)
+        HM[...] = jnp.maximum(HM[...], jnp.broadcast_to(peak, (8, 256)))
+        return 0
+
+    for s in range(2):
+        lax.fori_loop(4 * s, 4 * s + 4, fwd, 0)
+        for t in range(3, 5):
+            gd[s].pump(t)
+
+    class Scatter:
+        def __init__(self, i, s, partial):
+            self.i, self.s, self.partial = i, s, partial
+
+        def sib(self, slot):
+            return rcopy(SB.at[self.s, slot], SR.at[self.i, slot],
+                         rs_s.at[self.i, 8 + slot], rs_r.at[self.i, 8 + slot], sibling)
+
+        def produce(self):
+            def one(slot, _):
+                mag = 3 - (slot + 1) // 2 + 1
+                delta = mag * (2 * (slot % 2) - 1)
+                row = self.s * SL + 64 * ctx_of(r + delta, 0)
+                TMP[...] = self.partial(row)
+                LP[self.s, slot] = TMP[pl.ds(pl.multiple_of(64 * j, 64), 64), :]
+                SB[self.s, slot] = TMP[pl.ds(pl.multiple_of(64 * (1 - j), 64), 64), :].astype(bf16)
+                self.sib(slot).start()
+                return 0
+            lax.fori_loop(0, 8, one, 0)
+
+        def lane_sum(self, slot):
+            self.sib(slot).wait_recv()
+            return LP[self.s, slot] + SR[self.i, slot].astype(f32)
+
+        def ring(self, t, way):
+            slot = 4 * way + t
+            n = 32 if t == 0 else 64
+            return rcopy(RSB.at[self.s, slot, pl.ds(0, n)], RR.at[self.i, slot, pl.ds(0, n)],
+                         rs_s.at[self.i, slot], rs_r.at[self.i, slot], right if way == 0 else left)
+
+        def pump(self, t):
+            if t == 0:
+                v = self.lane_sum(0)
+                for way in (0, 1):
+                    RSB[self.s, 4 * way, 0:32, :] = v[32 * way:32 * way + 32].astype(bf16)
+                    self.ring(0, way).start()
+                return
+            for way in (0, 1):
+                v = self.lane_sum(2 * t - 1 + way)
+                self.ring(t - 1, way).wait_recv()
+                slot = 4 * way + t
+                if t == 1:
+                    got = RR[self.i, 4 * way, 0:32, :].astype(f32)
+                    if way == 0:
+                        RSB[self.s, slot, 0:32, :] = (v[0:32] + got).astype(bf16)
+                        RSB[self.s, slot, 32:64, :] = v[32:64].astype(bf16)
+                    else:
+                        RSB[self.s, slot, 0:32, :] = v[0:32].astype(bf16)
+                        RSB[self.s, slot, 32:64, :] = (v[32:64] + got).astype(bf16)
+                else:
+                    RSB[self.s, slot] = (v + RR[self.i, slot - 1].astype(f32)).astype(bf16)
+                self.ring(t, way).start()
+
+        def total(self):
+            v = self.lane_sum(7)
+            for way in (0, 1):
+                self.ring(3, way).wait_recv()
+                v = v + RR[self.i, 4 * way + 3].astype(f32)
+            return v
+
+        def drain(self):
+            for slot in range(8):
+                self.sib(slot).wait_send()
+            for t in range(4):
+                self.ring(t, 0).wait_send()
+                self.ring(t, 1).wait_send()
+
+    def out_partial(row):
+        return dot(AA[pl.ds(pl.multiple_of(row, 128), 128), :], WPD[...])
+
+    out = [Scatter(s, s, out_partial) for s in range(2)]
+    for s in range(2):
+        out[s].produce()
+        out[s].pump(0)
+    for s in range(2):
+        out[s].pump(1)
+
+    DSUM[d] = jnp.zeros((8, D), f32)
+
+    def dy_stage(i, _):
+        rows = pl.ds(pl.multiple_of(i * 128, 128), 128)
+        dyb = Y[rows, :]
+        back = dot_nt(dyb, WPD[...])
+        GG[rows, 256:512] = (back[:, 0:256] * GP[rows, :]).astype(bf16)
+        DA[rows, :] = back[:, 256:384].astype(bf16)
+        DSUM[d] += jnp.broadcast_to(jnp.sum(dyb.astype(f32), axis=0, keepdims=True), (8, D))
+        return 0
+
+    for s in range(2):
+        gd[s].finish()
+        lax.fori_loop(8 * s, 8 * s + 8, dy_stage, 0)
+        out[s].pump(2)
+    dm = rcopy(DSUM.at[d], DSUM.at[d], dm_s, dm_r, partner)
+    dm.start()
+
+    def bwd(i, _):
+        s = i // 4
+        rows = pl.ds(pl.multiple_of(i * 256, 256), 256)
+        seq = pl.ds(pl.multiple_of(s * SL, SL), SL)
+        q0 = pl.ds(pl.multiple_of((i % 4) * 256, 256), 256)
+        da = DA[rows, :]
+        rd = jnp.sum(da.astype(f32).T * ATT[i], axis=0, keepdims=True)
+        dpt = dot_nt(V[seq, :], da)
+        pt = PT[i]
+        ds = (pt.astype(f32) * (dpt - rd)).astype(bf16)
+        DV[...] += dot(pt, da)
+        DK[...] += dot(ds, Q[rows, :])
+        DQ[q0, :] = dot(KT[s], ds).T * 0.125
+        return 0
+
+    def qkv_back(i, s):
+        trow = pl.ds(pl.multiple_of(i * 128, 128), 128)
+        rows = pl.ds(pl.multiple_of(s * SL + i * 128, 128), 128)
+        both = DQ[trow, :] + pltpu.roll(DK[trow, :], 64, 1)
+        GG[rows, 0:128] = turn(both, CT[trow, :], ST[trow, :], -1.0).astype(bf16)
+        GG[rows, 128:256] = DV[trow, :].astype(bf16)
+        return s
+
+    GN[...] = jnp.zeros((8, D), f32)
+
+    def g_partial(row):
+        rows = pl.ds(pl.multiple_of(row, 128), 128)
+        nrm, _ = normed_of(X[rows, :])
+        gna = dot_nt(GG[rows, 0:256], WC[:, 0:256])
+        gnm = dot_nt(GG[rows, 256:512], WC[:, 256:512])
+        GN[0:1, :] += jnp.sum(gna * nrm, axis=0, keepdims=True)
+        GN[1:2, :] += jnp.sum(gna, axis=0, keepdims=True)
+        GN[2:3, :] += jnp.sum(gnm * nrm, axis=0, keepdims=True)
+        GN[3:4, :] += jnp.sum(gnm, axis=0, keepdims=True)
+        return gna * SM[0:1, :] + gnm * SM[2:3, :]
+
+    grad = [Scatter(2 + s, s, g_partial) for s in range(2)]
+
+    for s in range(2):
+        DV[...] = jnp.zeros((SL, 128), f32)
+        DK[...] = jnp.zeros((SL, 128), f32)
+        lax.fori_loop(4 * s, 4 * s + 4, bwd, 0)
+        lax.fori_loop(0, 8, qkv_back, s)
+        out[s].pump(3)
+        tot = out[s].total()
+        bo_ref[s * 64:s * 64 + 64, :] = (
+            x_ref[s * 64:s * 64 + 64, :].astype(f32) + tot + SM[4:5, :] + SM[5:6, :]
+        ).astype(bf16)
+        out[s].drain()
+        grad[s].produce()
+        grad[s].pump(0)
+
+    def transpose_aa(i, _):
+        rows = pl.ds(pl.multiple_of(i * 256, 256), 256)
+        TT[0:384, rows] = AA[rows, :].T
+        return 0
+
+    lax.fori_loop(0, 8, transpose_aa, 0)
+
+    def pd_grad(i, _):
+        cols = pl.ds(pl.multiple_of(i * 256, 256), 256)
+        PDS[:, cols] = dot(TT[0:384, :], Y[:, cols]).astype(bf16)
+        return 0
+
+    lax.fori_loop(0, 4, pd_grad, 0)
+
+    def gpd_copies(jj, slot_dp):
+        dev = (j, 2 * k + jj)
+        return (
+            rcopy(PDS.at[pl.ds(256 + 32 * jj, 32)], PDR.at[slot_dp, pl.ds(0, 32)],
+                  gpd_s.at[jj, 0], gpd_r.at[slot_dp, 0], dev),
+            rcopy(PDS.at[pl.ds(128 * jj, 128)], PDR.at[slot_dp, pl.ds(32, 128)],
+                  gpd_s.at[jj, 1], gpd_r.at[slot_dp, 1], dev),
+        )
+
+    for jj in range(2):
+        @pl.when(jnp.logical_not(here & (j == jj)))
+        def _():
+            for cp in gpd_copies(jj, d):
+                cp.start()
+
+    @pl.when(here)
+    def _():
+        PDR[d, 0:32, :] = PDS[pl.ds(256 + 32 * j, 32), :]
+        PDR[d, 32:160, :] = PDS[pl.ds(128 * j, 128), :]
+
+    for s in range(2):
+        grad[s].pump(1)
+
+    srow = jnp.zeros((1, 512), f32)
+    for i in range(TOK // 256):
+        srow = srow + jnp.sum(GG[i * 256:i * 256 + 256, :].astype(f32), axis=0, keepdims=True)
+    hmax = jnp.max(HM[...], axis=1, keepdims=True)[0:1, :]
+    SROW[...] = jnp.where(lane((1, 512)) == 192, hmax, srow)
+    me = NC * d + c
+    sr_ref[me] = SROW[...]
+
+    def s_copy(o, slot):
+        lin = (me + o) % 32
+        return rcopy(SROW, sr_ref.at[slot], sm_s.at[o], sm_r.at[o], (lin // NC, lin % NC))
+
+    def s_send(o, _):
+        s_copy(o, me).start()
+        return 0
+
+    lax.fori_loop(1, 32, s_send, 0)
+
+    def transpose_gg(i, _):
+        rows = pl.ds(pl.multiple_of(i * 256, 256), 256)
+        TT[:, rows] = GG[rows, :].T
+        return 0
+
+    lax.fori_loop(0, 8, transpose_gg, 0)
+
+    def in_grad(i, _):
+        cols = pl.ds(pl.multiple_of(i * 256, 256), 256)
+        a = dot(TT[0:256, :], NA[:, cols])
+        a = jnp.concatenate([a[0:192], GN[:, cols], a[200:256]], axis=0)
+        G[cols, 0:256] = a.T.astype(bf16)
+        G[cols, 256:512] = dot(TT[256:512, :], NM[:, cols]).T.astype(bf16)
+        return 0
+
+    lax.fori_loop(0, 4, in_grad, 0)
+    for s in range(2):
+        grad[s].pump(2)
+    gy = rcopy(G.at[other], GY, gy_s, gy_r, partner)
+    gy.start()
+    for s in range(2):
+        grad[s].pump(3)
+    gy.wait_recv()
+    GS[...] = (G[half, :].astype(f32) + GY[...].astype(f32)).astype(bf16)
+
+    def g_copy(o, dst_c, slot):
+        return rcopy(GS.at[pl.ds(pl.multiple_of(32 * dst_c, 32), 32)], gr_ref.at[slot],
+                     gg_s.at[o], gg_r.at[o], (d, dst_c))
+
+    def g_send(o, _):
+        g_copy(o, (c + o) % NC, head).start()
+        return 0
+
+    lax.fori_loop(1, NC, g_send, 0)
+    gr_ref[head] = GS[pl.ds(pl.multiple_of(32 * c, 32), 32), :]
+
+    for s in range(2):
+        tot = grad[s].total()
+        own = slice(s * 64, s * 64 + 64)
+        nrm, inv = normed_of(x_ref[own, :])
+        gh_ref[own, :] = (
+            dy_ref[own, :].astype(f32)
+            + inv * (tot - jnp.mean(tot, axis=1, keepdims=True)
+                     - nrm * jnp.mean(tot * nrm, axis=1, keepdims=True))
+        ).astype(bf16)
+
+    for e in range(2):
+        @pl.when(jnp.logical_not(here & (d == e)))
+        def _():
+            for cp in gpd_copies(0, e):
+                cp.wait_recv()
+    gp_ref[...] = PDR[0].astype(f32) + PDR[1].astype(f32)
+
+    rcopy(DSUM.at[1 - d], DSUM.at[1 - d], dm_s, dm_r, partner).wait_recv()
+    ds_ref[...] = DSUM[0] + DSUM[1]
+
+    def g_wait(o, _):
+        src_c = (c - o + NC) % NC
+        g_copy(o, (c + o) % NC, 8 * (src_c % 2) + src_c // 2).wait_recv()
+        return 0
+
+    lax.fori_loop(1, NC, g_wait, 0)
+
+    def s_wait(o, _):
+        s_copy(o, (me - o + 32) % 32).wait_recv()
+        return 0
+
+    lax.fori_loop(1, 32, s_wait, 0)
+
+    def w_done(o, _):
+        w_copy(o, (c + o) % NC, own_row).wait_send()
+        g_copy(o, (c + o) % NC, head).wait_send()
+        return 0
+
+    lax.fori_loop(1, NC, w_done, 0)
+
+    def s_done(o, _):
+        s_copy(o, me).wait_send()
+        return 0
+
+    lax.fori_loop(1, 32, s_done, 0)
+    wy.wait_send()
+    gy.wait_send()
+    dm.wait_send()
+    for e in range(2):
+        @pl.when(jnp.logical_not(here & (d == e)))
+        def _():
+            for cp in pd_copies(j, e):
+                cp.wait_send()
+
+        @pl.when(jnp.logical_not(here & (j == e)))
+        def _():
+            for cp in gpd_copies(e, d):
+                cp.wait_send()
+    for item in gx + gd + grad:
+        item.drain()
+
+
+def fast_shards(
+    hidden_in, out_cotangent, attn_gain, attn_shift, qkv_weight, qkv_bias, proj_weight, proj_bias,
+    mlp_gain, mlp_shift, up_weight, up_bias, down_weight, down_bias, picture_starts, group_order,
+):
+    rows = attn_gain.shape[0]
+    small = jnp.concatenate(
+        [
+            jnp.stack([attn_gain, attn_shift, mlp_gain, mlp_shift, proj_bias, down_bias], axis=1),
+            qkv_bias.reshape(rows, 3),
+            up_bias.reshape(rows, 4),
+            jnp.zeros((rows, 51), bf16),
+        ],
+        axis=1,
+    )
+    ws = jnp.concatenate(
+        [
+            qkv_weight.reshape(rows, 3, H, HD).transpose(2, 0, 1, 3).reshape(H, rows, 3 * HD),
+            jnp.broadcast_to(small[None], (H, rows, 64)),
+            up_weight.reshape(rows, H, 256).transpose(1, 0, 2),
+        ],
+        axis=2,
+    )
+    vm = pl.BlockSpec(memory_space=pltpu.VMEM)
+    sm = pl.BlockSpec(memory_space=pltpu.SMEM)
+    V_ = pltpu.VMEM
+    dma = pltpu.SemaphoreType.DMA
+    bo, gh, gr, gp, sr, ds = pl.pallas_call(
+        block_kernel,
+        out_shape=(
+            jax.ShapeDtypeStruct((128, D), bf16),
+            jax.ShapeDtypeStruct((128, D), bf16),
+            jax.ShapeDtypeStruct((NC, 32, 512), bf16),
+            jax.ShapeDtypeStruct((160, D), f32),
+            jax.ShapeDtypeStruct((32, 1, 512), f32),
+            jax.ShapeDtypeStruct((8, D), f32),
+        ),
+        in_specs=[sm, sm] + [vm] * 5,
+        out_specs=(vm,) * 6,
+        scratch_shapes=[
+            V_((TOK, D), bf16), V_((TOK, D), bf16), V_((TOK, D), bf16), V_((TOK, D), bf16),
+            V_((D, 512), bf16), V_((384, D), bf16),
+            V_((SL, 128), f32), V_((SL, 128), f32), V_((SL, 128), jnp.int32),
+            V_((2, 8, SL), jnp.int32), V_((16, D), f32), V_((2, 8, 256), f32),
+            V_((TOK, 128), bf16), V_((TOK, 128), bf16), V_((TOK, 128), bf16),
+            V_((2, 128, SL), bf16), V_((2, 128, SL), bf16),
+            V_((8, SL, 256), bf16), V_((8, 128, 256), f32),
+            V_((TOK, 384), bf16), V_((TOK, 256), f32), V_((TOK, 128), bf16), V_((TOK, 512), bf16),
+            V_((SL, 128), f32), V_((SL, 128), f32), V_((SL, 128), f32),
+            V_((8, 256), f32), V_((8, D), f32),
+            V_((512, TOK), bf16), V_((D, 512), bf16), V_((512, 512), bf16), V_((512, 512), bf16),
+            V_((384, D), bf16), V_((2, 160, D), bf16), V_((1, 512), f32), V_((2, 8, D), f32),
+            V_((128, D), f32), V_((2, 8, 64, D), f32), V_((2, 8, 64, D), bf16),
+            V_((2, 8, 64, D), bf16), V_((4, 8, 64, D), bf16), V_((4, 8, 64, D), bf16),
+            dma((NC,)), dma((NC,)), dma, dma, dma((2, 2)), dma((2, 2)), dma((4, 16)), dma((4, 16)),
+            dma((4, 16)), dma((4, 16)),
+            dma, dma, dma((NC,)), dma((NC,)), dma((2, 2)), dma((2, 2)), dma((32,)), dma((32,)), dma, dma,
+        ],
+        compiler_params=pltpu.CompilerParams(
+            collective_id=0, has_side_effects=True, vmem_limit_bytes=62 * 1024 * 1024
+        ),
+    )(
+        group_order, picture_starts, hidden_in.reshape(128, D), out_cotangent.reshape(128, D),
+        ws, proj_weight, down_weight,
+    )
+    me = NC * lax.axis_index("dp") + lax.axis_index("ctx")
+    grf = gr.astype(f32)
+    grad_qkv_weight = grf[:, :, :192].reshape(H, rows, 3, HD).transpose(1, 2, 0, 3).reshape(rows, 3 * D)
+    grad_up_weight = grf[:, :, 256:].transpose(1, 0, 2).reshape(rows, 4096)
+    gains = jnp.sum(grf[:, :, 192:196], axis=0)
+    tab = sr.reshape(2, 8, 2, 512).transpose(2, 1, 0, 3).reshape(H, 2, 512)
+    tsum = jnp.sum(tab, axis=1)
+    qkv_b = tsum[:, :192].reshape(H, 3, HD).transpose(1, 0, 2).reshape(3 * D)
+    up_b = tsum[:, 256:].reshape(4096)
+    head_max = jnp.max(tab[:, :, 192], axis=1)
+    grad_qkv_bias = lax.dynamic_slice(qkv_b, (96 * me,), (96,))
+    grad_up_bias = lax.dynamic_slice(up_b, (128 * me,), (128,))
+    grad_bias_out = lax.dynamic_slice(ds[0], (32 * me,), (32,))
+    clip_ratio = jnp.sqrt(clip_bound / jnp.maximum(head_max, clip_bound))
+    head_cols = jnp.repeat(clip_ratio, HD)
+    factor = jnp.concatenate([head_cols, head_cols, jnp.ones((D,), f32)])
+    clipped_qkv = qkv_weight.astype(f32) * factor[None, :]
+    return (
+        bo.reshape(2, 64, D), gh.reshape(2, 64, D), gains[:, 0], gains[:, 1],
+        grad_qkv_weight, grad_qkv_bias, gp[:32], grad_bias_out, gains[:, 2], gains[:, 3],
+        grad_up_weight, grad_up_bias, gp[32:], grad_bias_out, clipped_qkv,
+    )
+
+
 def solution(mesh):
     in_specs = (
         P("dp", "ctx", None),
@@ -442,4 +1143,5 @@
         P(("dp", "ctx")),
         P(("dp", "ctx"), None),
     )
-    return jax.shard_map(shards, mesh=mesh, in_specs=in_specs, out_specs=out_specs, check_vma=False)
+    body = fast_shards if (mesh.shape["dp"], mesh.shape["ctx"]) == (2, H) else shards
+    return jax.shard_map(body, mesh=mesh, in_specs=in_specs, out_specs=out_specs, check_vma=False)

time: 1470 us -> 181 us (0.12); the launches traced: 1450 us -> 180 us
  waiting for transfers between devices: 702 us -> 0 us
  local copies, waits for them, and re-layouts: 280 us -> 18.5 us
  matrix products: 225 us -> 0 us
  Pallas kernels: 0 us -> 157 us
  blocking collectives: 155 us -> 0 us
  loops' own time: 37.1 us -> 0 us
  other arithmetic: 36.1 us -> 3.29 us
    reduce_scatter x1 -> x0, waiting for transfers between devices: 460 us -> none  [shards(): lax.psum_scatter(jnp.concatenate([jnp.concatenate([proj_part, down_part,...]
    all_gather x8 -> x0, waiting for transfers between devices: 240 us -> none  [the longest x1 66.8 us: shards(): down_piece = lax.all_gather(down_rows, ('dp', 'ctx'), axis=0, tiled=True)]
    dot_general x124 -> x0, matrix products: 225 us -> none  [the longest x16 40.4 us: key_step(): jnp.einsum('bhqk,bqhd->bhkd', prob_rows.astype(bf16), grad_piece, preferr...]
    pallas_call x0 -> x1, Pallas kernels: none -> 157 us  [fast_shards(): pl.pallas_call(block_kernel, out_shape=(jax.ShapeDtypeStruct((128, D), bf...]
    all_gather x3 -> x0, blocking collectives: 92.9 us -> none  [the longest x1 43.8 us: shards(): small_piece = lax.all_gather(small_local, ('dp', 'ctx'), axis=0, tiled=True)]
    dynamic_slice x112 -> x3, local copies, waits for them, and re-layouts: 92.7 us -> 1.25 us  [the longest x1 0.59 us: fast_shards(): grad_up_bias = lax.dynamic_slice(up_b, (128 * me,), (128,))]
    reshape x109 -> x14, local copies, waits for them, and re-layouts: 77.6 us -> 4.45 us  [the longest x3 1.79 us: fast_shards(): qkv_weight.reshape(rows, 3, H, HD).transpose(2, 0, 1, 3)]
    concatenate x2 -> x1, local copies, waits for them, and re-layouts: 62.3 us -> 0.1 us  [fast_shards(): jnp.concatenate([jnp.stack([attn_gain, attn_shift, mlp_gain, mlp_shift, p...]
  transfers between devices with their start and end apart: 9 -> 0, of which waited for: 6 -> 0; matrix products, arithmetic and copies ran while one was open for 13% -> 0% of each run, Pallas kernels for 0% -> 0%
where the time goes in v1:
time: 181 us; the launch traced here: 180 us
  Pallas kernels  157 us (87%)
  local copies, waits for them, and re-layouts  18.5 us (10%)
  other arithmetic  3.29 us (2%)
    pallas_call x1, Pallas kernels, fast_shards(): pl.pallas_call(block_kernel, out_shape=(jax.ShapeDtypeStruct((128, D), bf...  157 us
    unnamed x36, local copies, waits for them, and re-layouts  8.55 us

profile of v1, /device:TPU:0, one launch (start us, length us, event | category | flops | bytes accessed | tf_op | source)
XLA Modules:
  0.0 180.0 jit_solution(8158261022421892021)
XLA Ops:
  0.7 1.2 reshape.90
  1.9 0.2 copy.94
  2.2 0.3 reshape.91
  2.5 0.6 copy-done.3
  3.1 0.6 copy-done.6
  3.9 0.7 copy-done.7
  4.6 0.7 copy-done.8
  5.4 0.7 copy-done.9
  6.2 0.7 copy-done.10
  6.9 0.7 copy-done.11
  7.7 0.6 copy-done.12
  8.3 0.5 copy-done.13
  9.1 1.0 pad_maximum_fusion.ws_ref
  10.1 157.3 %shard_map.271 = (bf16[128,1024]{1,0:T(8,128)(2,1)}, bf16[128,1024]{1,0:T(8,128)(2,1)}, bf16[16,32,512]{2,1,0:T(8,128)(2,1)}, f32[160,1024]{1,0:T(8,128)}, f32[32,1,512]{2,1,0:T(1,128)}, /*index=5*/f32[8,1024]{1,0:T(8,128)}) custom-call(s32[16]{0:T(128)} %go_ref.1, s32[2,4]{1,0:T(2,128)} %ps_ref.1, bf16[128,1024]{1,0:T(8,128)(2,1)} %bitcast.47, ...), custom_call_target="tpu_custom_call" | custom-call | tf_op jit(solution)/shard_map/pallas_call | solution.py:1048
  167.5 1.1 reduce.4
  168.8 0.6 dynamic_slice.11
  169.4 0.6 dynamic_slice.14
  170.0 0.8 slice.45
  171.1 0.7 slice_reduce_fusion.2
  171.8 0.8 copy.88
  172.7 0.3 reshape.97
  173.1 0.5 copy.82
  173.5 1.0 reshape.98
  174.5 0.2 slice_reduce_fusion.1
  174.9 0.6 copy-done.1
  175.5 0.8 convert_multiply_fusion
  176.2 0.8 slice.50
  177.1 0.7 slice.44
  177.7 0.5 copy.100
  178.2 0.7 copy.101
  179.0 0.3 copy-done.4
  179.3 0.7 copy.102
  (50 shorter events, 1.8 us)
Async XLA Ops:
  2.1 1.0 copy-start.3
  3.1 0.7 copy-start.6
  3.9 0.7 copy-start.7
  4.6 0.7 copy-start.8
  5.4 0.7 copy-start.9
  6.2 0.7 copy-start.10
  6.9 0.7 copy-start.11
  7.6 0.7 copy-start.12
  8.2 0.7 copy-start.13
  167.5 3.3 %copy-start = (bf16[16,32,512]{2,1,0:T(8,128)(2,1)S(1)}, bf16[16,32,512]{2,1,0:T(8,128)(2,1)}, u32[]{:S(2)}) copy-start(bf16[16,32,512]{2,1,0:T(8,128)(2,1)} %get-tuple-element.23) | copy-start | bytes 1572868
  170.8 6.9 %copy-start.14 = (f32[32]{0:T(128)}, f32[32]{0:T(128)S(1)}, u32[]{:S(2)}) copy-start(f32[32]{0:T(128)S(1)} %dynamic-slice_bitcast_fusion) | copy-start | bytes 388
  173.5 2.7 %copy-start.2 = (f32[160,1024]{1,0:T(8,128)S(1)}, f32[160,1024]{1,0:T(8,128)}, u32[]{:S(2)}) copy-start(f32[160,1024]{1,0:T(8,128)} %get-tuple-element.25) | copy-start | bytes 1966084
  174.5 0.9 copy-start.1
  177.1 1.2 copy-start.5
  178.2 1.0 copy-start.4

commit v2 on v1

--- a/solution.py
+++ b/solution.py
@@ -428,13 +428,15 @@
 
 
 def block_kernel(
-    go_ref, ps_ref, x_ref, dy_ref, ws_ref, pw_ref, dw_ref,
-    bo_ref, gh_ref, gr_ref, gp_ref, sr_ref, ds_ref,
+    go_ref, ps_ref, x_ref, dy_ref, qw_ref, uw_ref, pw_ref, dw_ref,
+    ag_ref, as_ref, mg_ref, ms_ref, pb_ref, db_ref, qb_ref, ub_ref,
+    bo_ref, gh_ref, gra_ref, grb_ref, gp_ref, sr_ref, ds_ref,
+    QW, UW, V0, V1, V2, V3, V4, V5, V6, V7, WS,
     X, Y, NA, NM, WC, WPD, CT, ST, PK, LIM, SM, BV,
     Q, K, V, VT, KT, PT, ATT, AA, GP, DA, GG, DQ, DK, DV, HM, GN,
-    TT, G, GY, GS, PDS, PDR, SROW, DSUM,
+    TT, GA, GB, GYA, GYB, GSA, GSB, PDS, PDR, SROW, DSUM,
     TMP, LP, SB, RSB, SR, RR,
-    w_s, w_r, wy_s, wy_r, pd_s, pd_r, ga_s, ga_r, rs_s, rs_r,
+    in_s, w_s, w_r, wy_s, wy_r, pd_s, pd_r, ga_s, ga_r, rs_s, rs_r,
     gy_s, gy_r, gg_s, gg_r, gpd_s, gpd_r, sm_s, sm_r, dm_s, dm_r,
 ):
     d = lax.axis_index("dp")
@@ -468,11 +470,53 @@
         return 0
 
     lax.fori_loop(1, 32, hello, 0)
+
+    def own_rows(s):
+        return pl.ds(pl.multiple_of(s * SL + 64 * c, 64), 64)
+
+    vecs = (V0, V1, V2, V3, V4, V5, V6, V7)
+    fetch = [pltpu.make_async_copy(qw_ref, QW, in_s.at[0]), pltpu.make_async_copy(uw_ref, UW, in_s.at[1])]
+    for i, ref in enumerate((ag_ref, as_ref, mg_ref, ms_ref, pb_ref, db_ref)):
+        fetch.append(pltpu.make_async_copy(ref, vecs[i], in_s.at[2 + i]))
+    fetch.append(pltpu.make_async_copy(qb_ref, vecs[6], in_s.at[8]))
+    fetch.append(pltpu.make_async_copy(ub_ref, vecs[7], in_s.at[9]))
+    fetch_x = [pltpu.make_async_copy(x_ref.at[s], X.at[own_rows(s)], in_s.at[10 + s]) for s in range(2)]
+    fetch_y = [pltpu.make_async_copy(dy_ref.at[s], Y.at[own_rows(s)], in_s.at[12 + s]) for s in range(2)]
+    for cp in fetch + fetch_x + fetch_y:
+        cp.start()
+    for cp in fetch:
+        cp.wait()
+
+    def lane(shape):
+        return lax.broadcasted_iota(jnp.int32, shape, len(shape) - 1)
+
+    TMP[:, 0:128] = jnp.zeros((128, 128), f32)
+    for i in range(6):
+        TMP[64 + i:65 + i, 0:32] = vecs[i][...].astype(f32)
+    TMP[0:1, 0:96] = V6[...].astype(f32)
+    vq, vu = TMP[0:1, 0:128], V7[...].astype(f32)
+    for i in range(3):
+        TMP[70 + i:71 + i, 0:128] = pltpu.roll(vq, (128 - 32 * i) % 128, 1)
+    for i in range(4):
+        TMP[73 + i:74 + i, 0:128] = pltpu.roll(vu, (128 - 32 * i) % 128, 1)
+    vcols = TMP[:, 0:128].T[0:32, :]
+    low32 = lane((32, 128)) < 64
+    for hp in range(H // 2):
+        q2 = QW[:, 128 * hp:128 * hp + 128].astype(f32)
+        k2 = QW[:, D + 128 * hp:D + 128 * hp + 128].astype(f32)
+        v2 = QW[:, 2 * D + 128 * hp:2 * D + 128 * hp + 128].astype(f32)
+        WS[2 * hp, :, 0:128] = jnp.where(low32, q2, pltpu.roll(k2, 64, 1)).astype(bf16)
+        WS[2 * hp + 1, :, 0:128] = jnp.where(low32, pltpu.roll(q2, 64, 1), k2).astype(bf16)
+        WS[2 * hp, :, 128:256] = jnp.where(low32, v2, vcols).astype(bf16)
+        WS[2 * hp + 1, :, 128:256] = jnp.where(low32, pltpu.roll(v2, 64, 1), vcols).astype(bf16)
+    for h in range(H):
+        WS[h, :, 256:512] = UW[:, 256 * h:256 * h + 256]
+
     pl.semaphore_wait(barrier, 31)
 
     def w_copy(o, dst_c, row):
         return rcopy(
-            ws_ref.at[8 * (dst_c % 2) + dst_c // 2],
+            WS.at[8 * (dst_c % 2) + dst_c // 2],
             WC.at[pl.ds(pl.multiple_of(row, 32), 32)],
             w_s.at[o], w_r.at[o], (d, dst_c),
         )
@@ -484,6 +528,14 @@
         return 0
 
     lax.fori_loop(1, NC, w_send, 0)
+    WC[pl.ds(pl.multiple_of(own_row, 32), 32), :] = WS[head]
+
+    def wy_copy(o, plane):
+        row = 32 * (NC * plane + (c - o + NC) % NC)
+        region = WC.at[pl.ds(pl.multiple_of(row, 32), 32)]
+        return rcopy(region, region, wy_s.at[o], wy_r.at[o], partner)
+
+    wy_copy(0, d).start()
 
     class Gather:
         def __init__(self, buf, own, s, i):
@@ -513,8 +565,7 @@
             return rcopy(region, region, ga_s.at[self.i, 8 + slot], ga_r.at[self.i, 8 + slot], sibling)
 
         def start(self):
-            row = self.s * SL + 64 * c
-            self.buf[pl.ds(pl.multiple_of(row, 64), 64), :] = self.own[self.s * 64:self.s * 64 + 64, :]
+            self.own[self.s].wait()
             self.ring(0, 0).start()
             self.ring(0, 1).start()
             self.sib(0, j).start()
@@ -528,8 +579,8 @@
             if t == 4:
                 self.sib(7, j).start()
 
-        def finish(self):
-            for slot in range(8):
+        def ready(self, t):
+            for slot in ((0,) if t == 0 else (t, 3 + t) if t < 4 else (7,)):
                 self.sib(slot, 1 - j).wait_recv()
 
         def drain(self):
@@ -539,8 +590,8 @@
             for slot in range(8):
                 self.sib(slot, j).wait_send()
 
-    gx = [Gather(X, x_ref, s, s) for s in range(2)]
-    gd = [Gather(Y, dy_ref, s, 2 + s) for s in range(2)]
+    gx = [Gather(X, fetch_x, s, s) for s in range(2)]
+    gd = [Gather(Y, fetch_y, s, 2 + s) for s in range(2)]
     gx[0].start()
     gx[1].start()
 
@@ -552,22 +603,24 @@
         )
 
     here = d == j
-    for e in range(2):
-        @pl.when(jnp.logical_not(here & (d == e)))
-        def _():
-            for cp in pd_copies(j, e):
-                cp.start()
+
+    def pd_start():
+        for e in range(2):
+            @pl.when(jnp.logical_not(here & (d == e)))
+            def _():
+                for cp in pd_copies(j, e):
+                    cp.start()
+
+    local_pd = (
+        pltpu.make_async_copy(pw_ref, WPD.at[pl.ds(256 + 32 * j, 32)], in_s.at[14]),
+        pltpu.make_async_copy(dw_ref, WPD.at[pl.ds(128 * j, 128)], in_s.at[15]),
+    )
 
     @pl.when(here)
     def _():
-        WPD[pl.ds(256 + 32 * j, 32), :] = pw_ref[...]
-        WPD[pl.ds(128 * j, 128), :] = dw_ref[...]
+        for cp in local_pd:
+            cp.start()
     WPD[320:384, :] = jnp.zeros((64, D), bf16)
-
-    WC[pl.ds(pl.multiple_of(own_row, 32), 32), :] = ws_ref[head]
-
-    def lane(shape):
-        return lax.broadcasted_iota(jnp.int32, shape, len(shape) - 1)
 
     rows_i = lax.broadcasted_iota(jnp.int32, (SL, 128), 0)
     place = jnp.zeros((SL, 128), jnp.int32)
@@ -608,23 +661,19 @@
     def w_wait(o, _):
         src_c = (c - o + NC) % NC
         w_copy(o, (c + o) % NC, 32 * (NC * d + src_c)).wait_recv()
+        wy_copy(o, d).start()
         return 0
 
     lax.fori_loop(1, NC, w_wait, 0)
-    wy = rcopy(WC.at[half], WC.at[half], wy_s, wy_r, partner)
-    wy.start()
-    for t in range(1, 5):
-        gx[0].pump(t)
-        gx[1].pump(t)
-    gd[0].start()
-    gd[1].start()
-    rcopy(WC.at[other], WC.at[other], wy_s, wy_r, partner).wait_recv()
-
-    for jj in range(2):
-        @pl.when(jnp.logical_not(here & (j == jj)))
-        def _():
-            for cp in pd_copies(jj, 0):
-                cp.wait_recv()
+    pd_start()
+    gx[0].pump(1)
+    gx[1].pump(1)
+
+    def wy_wait(o, _):
+        wy_copy(o, 1 - d).wait_recv()
+        return 0
+
+    lax.fori_loop(0, NC, wy_wait, 0)
 
     SM[...] = WC[:, 128:256].astype(f32).T[64:80, :]
     en = lane((16, 256))
@@ -634,18 +683,23 @@
     smb = SM[...].astype(bf16)
 
     def pick(e_big, e_small, div, first):
-        n_big = div(e_big)
-        onehot = jnp.where(feat == n_big, 1.0, 0.0).astype(bf16)
+        onehot = jnp.where(feat == div(e_big)[0], 1.0, 0.0).astype(bf16)
         got = dot(smb, onehot)
-        width = 3 if first == 6 else 4
-        return jnp.sum(jnp.where(vrow == first + e_small - width * div(e_small), got, 0.0), axis=0, keepdims=True)
+        return jnp.sum(jnp.where(vrow == first + div(e_small)[1], got, 0.0), axis=0, keepdims=True)
+
+    def place_qkv(e):
+        owner = ((e >> 5) * 171) >> 9
+        return 32 * owner + (e & 31), (e >> 5) - 3 * owner
+
+    def place_up(e):
+        return 32 * (e >> 7) + (e & 31), (e >> 5) & 3
 
     def e_qkv(ln):
         return SL * (ln >> 6) + HD * head + (ln & 63)
 
-    bq = pick(e_qkv(jl), e_qkv(en), lambda e: (e * 43691) >> 17, 6)
+    bq = pick(e_qkv(jl), e_qkv(en), place_qkv, 6)
     bq = jnp.where(lane((1, 256)) < 192, bq, 0.0)
-    bu = pick(256 * head + jl, 256 * head + en, lambda e: e >> 2, 9)
+    bu = pick(256 * head + jl, 256 * head + en, place_up, 9)
     BV[0] = jnp.broadcast_to(bq, (8, 256))
     BV[1] = jnp.broadcast_to(bu, (8, 256))
 
@@ -682,11 +736,42 @@
         GP[rows, :] = cdf + up * (jnp.exp(-0.5 * up * up) * ((2.0 * math.pi) ** -0.5))
         return 0
 
-    for s in range(2):
-        gx[s].finish()
-        lax.fori_loop(8 * s, 8 * s + 8, n_stage, 0)
-        for t in range(1, 3):
-            gd[s].pump(t)
+    def n_blocks(t):
+        for s in range(2):
+            gx[s].ready(t)
+        count = 2 if t in (0, 4) else 4
+
+        def one(i, _):
+            s = i % 2
+            delta = t * (1 - 2 * (i // 2))
+            return n_stage(8 * s + ctx_of(r + delta, 0) // 2, 0)
+
+        lax.fori_loop(0, count, one, 0)
+
+    def dy_blocks(s, t):
+        gd[s].ready(t)
+        count = 1 if t in (0, 4) else 2
+
+        def one(i, _):
+            return dy_stage(8 * s + ctx_of(r + t * (1 - 2 * i), 0) // 2, 0)
+
+        lax.fori_loop(0, count, one, 0)
+
+    n_blocks(0)
+    gx[0].pump(2)
+    gx[1].pump(2)
+    n_blocks(1)
+    gd[0].start()
+    gx[0].pump(3)
+    gx[1].pump(3)
+    n_blocks(2)
+    gd[1].start()
+    gx[0].pump(4)
+    gx[1].pump(4)
+    n_blocks(3)
+    gd[0].pump(1)
+    n_blocks(4)
+    gd[1].pump(1)
 
     for s in range(2):
         VT[s] = V[s * SL:s * SL + SL, :].astype(f32).T.astype(bf16)
@@ -713,11 +798,6 @@
         AA[rows, 256:384] = at.T.astype(bf16)
         HM[...] = jnp.maximum(HM[...], jnp.broadcast_to(peak, (8, 256)))
         return 0
-
-    for s in range(2):
-        lax.fori_loop(4 * s, 4 * s + 4, fwd, 0)
-        for t in range(3, 5):
-            gd[s].pump(t)
 
     class Scatter:
         def __init__(self, i, s, partial):
@@ -790,12 +870,6 @@
         return dot(AA[pl.ds(pl.multiple_of(row, 128), 128), :], WPD[...])
 
     out = [Scatter(s, s, out_partial) for s in range(2)]
-    for s in range(2):
-        out[s].produce()
-        out[s].pump(0)
-    for s in range(2):
-        out[s].pump(1)
-
     DSUM[d] = jnp.zeros((8, D), f32)
 
     def dy_stage(i, _):
@@ -806,13 +880,6 @@
         DA[rows, :] = back[:, 256:384].astype(bf16)
         DSUM[d] += jnp.broadcast_to(jnp.sum(dyb.astype(f32), axis=0, keepdims=True), (8, D))
         return 0
-
-    for s in range(2):
-        gd[s].finish()
-        lax.fori_loop(8 * s, 8 * s + 8, dy_stage, 0)
-        out[s].pump(2)
-    dm = rcopy(DSUM.at[d], DSUM.at[d], dm_s, dm_r, partner)
-    dm.start()
 
     def bwd(i, _):
         s = i // 4
@@ -852,19 +919,97 @@
 
     grad = [Scatter(2 + s, s, g_partial) for s in range(2)]
 
-    for s in range(2):
+    def out_done(s):
+        tot = out[s].total()
+        bo_ref[s * 64:s * 64 + 64, :] = (
+            X[own_rows(s), :].astype(f32) + tot + SM[4:5, :] + SM[5:6, :]
+        ).astype(bf16)
+        out[s].drain()
+
+    def bwd_start():
         DV[...] = jnp.zeros((SL, 128), f32)
         DK[...] = jnp.zeros((SL, 128), f32)
-        lax.fori_loop(4 * s, 4 * s + 4, bwd, 0)
-        lax.fori_loop(0, 8, qkv_back, s)
-        out[s].pump(3)
-        tot = out[s].total()
-        bo_ref[s * 64:s * 64 + 64, :] = (
-            x_ref[s * 64:s * 64 + 64, :].astype(f32) + tot + SM[4:5, :] + SM[5:6, :]
-        ).astype(bf16)
-        out[s].drain()
-        grad[s].produce()
-        grad[s].pump(0)
+
+    gd[0].pump(2)
+    lax.fori_loop(0, 2, fwd, 0)
+    for jj in range(2):
+        @pl.when(jnp.logical_not(here & (j == jj)))
+        def _():
+            for cp in pd_copies(jj, 0):
+                cp.wait_recv()
+
+    @pl.when(here)
+    def _():
+        for cp in local_pd:
+            cp.wait()
+
+    gd[1].pump(2)
+    lax.fori_loop(2, 4, fwd, 0)
+    gd[0].pump(3)
+    out[0].produce()
+    out[0].pump(0)
+    gd[1].pump(3)
+    lax.fori_loop(4, 6, fwd, 0)
+    gd[0].pump(4)
+    out[0].pump(1)
+    lax.fori_loop(6, 8, fwd, 0)
+    gd[1].pump(4)
+    out[1].produce()
+    out[1].pump(0)
+    out[0].pump(2)
+    for t in range(5):
+        dy_blocks(0, t)
+    out[1].pump(1)
+    for t in range(5):
+        dy_blocks(1, t)
+    dm = rcopy(DSUM.at[d], DSUM.at[d], dm_s, dm_r, partner)
+    dm.start()
+    out[0].pump(3)
+    out[1].pump(2)
+    bwd_start()
+    lax.fori_loop(0, 4, bwd, 0)
+    lax.fori_loop(0, 8, qkv_back, 0)
+    out[1].pump(3)
+    out_done(0)
+    grad[0].produce()
+    grad[0].pump(0)
+    bwd_start()
+    lax.fori_loop(4, 6, bwd, 0)
+    grad[0].pump(1)
+    out_done(1)
+    lax.fori_loop(6, 8, bwd, 0)
+    grad[0].pump(2)
+    lax.fori_loop(0, 8, qkv_back, 1)
+    grad[1].produce()
+    grad[1].pump(0)
+    grad[0].pump(3)
+
+    def transpose_gg(i, _):
+        rows = pl.ds(pl.multiple_of(i * 256, 256), 256)
+        TT[:, rows] = GG[rows, :].T
+        return 0
+
+    lax.fori_loop(0, 8, transpose_gg, 0)
+
+    def qkv_grad(i, _):
+        cols = pl.ds(pl.multiple_of(i * 256, 256), 256)
+        a = dot(TT[0:256, :], NA[:, cols])
+        a = jnp.concatenate([a[0:192], GN[:, cols], a[200:256]], axis=0)
+        GA[cols, :] = a.T.astype(bf16)
+        return 0
+
+    def up_grad(i, _):
+        cols = pl.ds(pl.multiple_of(i * 256, 256), 256)
+        GB[cols, :] = dot(TT[256:512, :], NM[:, cols]).T.astype(bf16)
+        return 0
+
+    lax.fori_loop(0, 4, qkv_grad, 0)
+    gya = rcopy(GA.at[other], GYA, gy_s.at[0], gy_r.at[0], partner)
+    gya.start()
+    grad[1].pump(1)
+    lax.fori_loop(0, 4, up_grad, 0)
+    gyb = rcopy(GB.at[other], GYB, gy_s.at[1], gy_r.at[1], partner)
+    gyb.start()
 
     def transpose_aa(i, _):
         rows = pl.ds(pl.multiple_of(i * 256, 256), 256)
@@ -900,8 +1045,7 @@
         PDR[d, 0:32, :] = PDS[pl.ds(256 + 32 * j, 32), :]
         PDR[d, 32:160, :] = PDS[pl.ds(128 * j, 128), :]
 
-    for s in range(2):
-        grad[s].pump(1)
+    grad[1].pump(2)
 
     srow = jnp.zeros((1, 512), f32)
     for i in range(TOK // 256):
@@ -921,48 +1065,29 @@
 
     lax.fori_loop(1, 32, s_send, 0)
 
-    def transpose_gg(i, _):
-        rows = pl.ds(pl.multiple_of(i * 256, 256), 256)
-        TT[:, rows] = GG[rows, :].T
-        return 0
-
-    lax.fori_loop(0, 8, transpose_gg, 0)
-
-    def in_grad(i, _):
-        cols = pl.ds(pl.multiple_of(i * 256, 256), 256)
-        a = dot(TT[0:256, :], NA[:, cols])
-        a = jnp.concatenate([a[0:192], GN[:, cols], a[200:256]], axis=0)
-        G[cols, 0:256] = a.T.astype(bf16)
-        G[cols, 256:512] = dot(TT[256:512, :], NM[:, cols]).T.astype(bf16)
-        return 0
-
-    lax.fori_loop(0, 4, in_grad, 0)
-    for s in range(2):
-        grad[s].pump(2)
-    gy = rcopy(G.at[other], GY, gy_s, gy_r, partner)
-    gy.start()
-    for s in range(2):
-        grad[s].pump(3)
-    gy.wait_recv()
-    GS[...] = (G[half, :].astype(f32) + GY[...].astype(f32)).astype(bf16)
-
-    def g_copy(o, dst_c, slot):
-        return rcopy(GS.at[pl.ds(pl.multiple_of(32 * dst_c, 32), 32)], gr_ref.at[slot],
-                     gg_s.at[o], gg_r.at[o], (d, dst_c))
-
-    def g_send(o, _):
-        g_copy(o, (c + o) % NC, head).start()
-        return 0
-
-    lax.fori_loop(1, NC, g_send, 0)
-    gr_ref[head] = GS[pl.ds(pl.multiple_of(32 * c, 32), 32), :]
+    def g_copy(half_i, o, dst_c, slot):
+        src, dst = ((GSA, gra_ref), (GSB, grb_ref))[half_i]
+        return rcopy(src.at[pl.ds(pl.multiple_of(32 * dst_c, 32), 32)], dst.at[slot],
+                     gg_s.at[half_i, o], gg_r.at[half_i, o], (d, dst_c))
+
+    for half_i, (gy, G, GY, GS, gr_ref) in enumerate(((gya, GA, GYA, GSA, gra_ref), (gyb, GB, GYB, GSB, grb_ref))):
+        gy.wait_recv()
+        GS[...] = (G[half, :].astype(f32) + GY[...].astype(f32)).astype(bf16)
+
+        def g_send(o, _):
+            g_copy(half_i, o, (c + o) % NC, head).start()
+            return 0
+
+        lax.fori_loop(1, NC, g_send, 0)
+        gr_ref[head] = GS[pl.ds(pl.multiple_of(32 * c, 32), 32), :]
+    grad[1].pump(3)
 
     for s in range(2):
         tot = grad[s].total()
         own = slice(s * 64, s * 64 + 64)
-        nrm, inv = normed_of(x_ref[own, :])
+        nrm, inv = normed_of(X[own_rows(s), :])
         gh_ref[own, :] = (
-            dy_ref[own, :].astype(f32)
+            Y[own_rows(s), :].astype(f32)
             + inv * (tot - jnp.mean(tot, axis=1, keepdims=True)
                      - nrm * jnp.mean(tot * nrm, axis=1, keepdims=True))
         ).astype(bf16)
@@ -979,7 +1104,8 @@
 
     def g_wait(o, _):
         src_c = (c - o + NC) % NC
-        g_copy(o, (c + o) % NC, 8 * (src_c % 2) + src_c // 2).wait_recv()
+        for half_i in range(2):
+            g_copy(half_i, o, (c + o) % NC, 8 * (src_c % 2) + src_c // 2).wait_recv()
         return 0
 
     lax.fori_loop(1, NC, g_wait, 0)
@@ -992,7 +1118,9 @@
 
     def w_done(o, _):
         w_copy(o, (c + o) % NC, own_row).wait_send()
-        g_copy(o, (c + o) % NC, head).wait_send()
+        for half_i in range(2):
+            g_copy(half_i, o, (c + o) % NC, head).wait_send()
+        wy_copy(o, d).wait_send()
         return 0
 
     lax.fori_loop(1, NC, w_done, 0)
@@ -1002,8 +1130,9 @@
         return 0
 
     lax.fori_loop(1, 32, s_done, 0)
-    wy.wait_send()
-    gy.wait_send()
+    wy_copy(0, d).wait_send()
+    gya.wait_send()
+    gyb.wait_send()
     dm.wait_send()
     for e in range(2):
         @pl.when(jnp.logical_not(here & (d == e)))
@@ -1019,45 +1148,89 @@
         item.drain()
 
 
+def finish_kernel(
+    bo, gh, gra, grb, gp, sr, ds, qw,
+    o_bo, o_gh, o_ag, o_as, o_qw, o_qb, o_pw, o_pb, o_mg, o_ms, o_uw, o_ub, o_dw, o_db, o_cq,
+    B, F,
+):
+    me = NC * lax.axis_index("dp") + lax.axis_index("ctx")
+    for s in range(2):
+        o_bo[s] = bo[64 * s:64 * s + 64, :]
+        o_gh[s] = gh[64 * s:64 * s + 64, :]
+    o_pw[...] = gp[0:32, :]
+    o_dw[...] = gp[32:160, :]
+    low = lax.broadcasted_iota(jnp.int32, (32, 128), 1) < 64
+    low1 = low[0:1]
+    gains = jnp.zeros((32, 128), f32)
+    for h in range(H):
+        at = 2 * (h % 8) + h // 8
+        one, two = sr[at], sr[NC + at]
+        both = one + two
+        peak = jnp.maximum(one, two)
+        col = lax.broadcasted_iota(jnp.int32, (1, 512), 1)
+        B[h:h + 1, :] = jnp.where(col == 192, peak, both)
+        F[32 + 2 * h:33 + 2 * h, :] = both[:, 256:384]
+        F[33 + 2 * h:34 + 2 * h, :] = both[:, 384:512]
+        gains = gains + gra[h, :, 128:256].astype(f32)
+        o_uw[:, 256 * h:256 * h + 256] = grb[h].astype(f32)
+    top = B[:, 128:256]
+    top = jnp.max(jnp.where(lax.broadcasted_iota(jnp.int32, (H, 128), 1) == 64, top, masked_score), axis=1, keepdims=True)
+    ratio = jnp.broadcast_to(jnp.sqrt(clip_bound / jnp.maximum(top, clip_bound)), (H, 128))
+    F[24:32, :] = jnp.zeros((8, 128), f32)
+    for hp in range(H // 2):
+        a, b = gra[2 * hp, :, 0:128].astype(f32), gra[2 * hp + 1, :, 0:128].astype(f32)
+        va, vb = gra[2 * hp, :, 128:256].astype(f32), gra[2 * hp + 1, :, 128:256].astype(f32)
+        o_qw[:, 128 * hp:128 * hp + 128] = jnp.where(low, a, pltpu.roll(b, 64, 1))
+        o_qw[:, D + 128 * hp:D + 128 * hp + 128] = jnp.where(low, pltpu.roll(a, 64, 1), b)
+        o_qw[:, 2 * D + 128 * hp:2 * D + 128 * hp + 128] = jnp.where(low, va, pltpu.roll(vb, 64, 1))
+        ra, rb = B[2 * hp:2 * hp + 1, 0:128], B[2 * hp + 1:2 * hp + 2, 0:128]
+        sa, sb = B[2 * hp:2 * hp + 1, 128:256], B[2 * hp + 1:2 * hp + 2, 128:256]
+        F[hp:hp + 1, :] = jnp.where(low1, ra, pltpu.roll(rb, 64, 1))
+        F[8 + hp:9 + hp, :] = jnp.where(low1, pltpu.roll(ra, 64, 1), rb)
+        F[16 + hp:17 + hp, :] = jnp.where(low1, sa, pltpu.roll(sb, 64, 1))
+        fac = jnp.where(low1, ratio[2 * hp:2 * hp + 1], ratio[2 * hp + 1:2 * hp + 2])
+        for part in range(3):
+            cols = slice(part * D + 128 * hp, part * D + 128 * hp + 128)
+            w = qw[:, cols].astype(f32)
+            o_cq[:, cols] = w * fac if part < 2 else w
+    grows = jnp.concatenate([gains, jnp.zeros((96, 128), f32)], axis=0).T
+    for i, o in enumerate((o_ag, o_as, o_mg, o_ms)):
+        o[...] = grows[64 + i:65 + i, 0:32]
+    row, shift = (96 * me) // 128, (96 * me) % 128
+    turned = pltpu.roll(F[pl.ds(row, 1), :], (128 - shift) % 128, 1)
+    after = pltpu.roll(F[pl.ds(row + 1, 1), :], (128 - shift) % 128, 1)
+    col = lax.broadcasted_iota(jnp.int32, (1, 128), 1)
+    o_qb[...] = jnp.where(col < 128 - shift, turned, after)[:, 0:96]
+    o_ub[...] = F[pl.ds(32 + me, 1), :]
+    dsum = ds[0:1, pl.ds(pl.multiple_of(128 * (me // 4), 128), 128)]
+    dsum = pltpu.roll(dsum, (128 - 32 * (me % 4)) % 128, 1)[:, 0:32]
+    o_pb[...] = dsum
+    o_db[...] = dsum
+
+
 def fast_shards(
     hidden_in, out_cotangent, attn_gain, attn_shift, qkv_weight, qkv_bias, proj_weight, proj_bias,
     mlp_gain, mlp_shift, up_weight, up_bias, down_weight, down_bias, picture_starts, group_order,
 ):
-    rows = attn_gain.shape[0]
-    small = jnp.concatenate(
-        [
-            jnp.stack([attn_gain, attn_shift, mlp_gain, mlp_shift, proj_bias, down_bias], axis=1),
-            qkv_bias.reshape(rows, 3),
-            up_bias.reshape(rows, 4),
-            jnp.zeros((rows, 51), bf16),
-        ],
-        axis=1,
-    )
-    ws = jnp.concatenate(
-        [
-            qkv_weight.reshape(rows, 3, H, HD).transpose(2, 0, 1, 3).reshape(H, rows, 3 * HD),
-            jnp.broadcast_to(small[None], (H, rows, 64)),
-            up_weight.reshape(rows, H, 256).transpose(1, 0, 2),
-        ],
-        axis=2,
-    )
     vm = pl.BlockSpec(memory_space=pltpu.VMEM)
     sm = pl.BlockSpec(memory_space=pltpu.SMEM)
+    hbm = pl.BlockSpec(memory_space=pl.ANY)
     V_ = pltpu.VMEM
     dma = pltpu.SemaphoreType.DMA
-    bo, gh, gr, gp, sr, ds = pl.pallas_call(
+
+    def sds(shape, dtype=f32):
+        return jax.ShapeDtypeStruct(shape, dtype)
+
+    got = pl.pallas_call(
         block_kernel,
         out_shape=(
-            jax.ShapeDtypeStruct((128, D), bf16),
-            jax.ShapeDtypeStruct((128, D), bf16),
-            jax.ShapeDtypeStruct((NC, 32, 512), bf16),
-            jax.ShapeDtypeStruct((160, D), f32),
-            jax.ShapeDtypeStruct((32, 1, 512), f32),
-            jax.ShapeDtypeStruct((8, D), f32),
+            sds((128, D), bf16), sds((128, D), bf16), sds((NC, 32, 256), bf16), sds((NC, 32, 256), bf16),
+            sds((160, D)), sds((32, 1, 512)), sds((8, D)),
         ),
-        in_specs=[sm, sm] + [vm] * 5,
-        out_specs=(vm,) * 6,
+        in_specs=[sm, sm] + [hbm] * 14,
+        out_specs=(vm,) * 7,
         scratch_shapes=[
+            V_((32, 3 * D), bf16), V_((32, 4 * D), bf16), *(V_((1, n), bf16) for n in (32,) * 6 + (96, 128)), V_((NC, 32, 512), bf16),
             V_((TOK, D), bf16), V_((TOK, D), bf16), V_((TOK, D), bf16), V_((TOK, D), bf16),
             V_((D, 512), bf16), V_((384, D), bf16),
             V_((SL, 128), f32), V_((SL, 128), f32), V_((SL, 128), jnp.int32),
@@ -1068,43 +1241,35 @@
             V_((TOK, 384), bf16), V_((TOK, 256), f32), V_((TOK, 128), bf16), V_((TOK, 512), bf16),
             V_((SL, 128), f32), V_((SL, 128), f32), V_((SL, 128), f32),
             V_((8, 256), f32), V_((8, D), f32),
-            V_((512, TOK), bf16), V_((D, 512), bf16), V_((512, 512), bf16), V_((512, 512), bf16),
+            V_((512, TOK), bf16), V_((D, 256), bf16), V_((D, 256), bf16),
+            V_((512, 256), bf16), V_((512, 256), bf16), V_((512, 256), bf16), V_((512, 256), bf16),
             V_((384, D), bf16), V_((2, 160, D), bf16), V_((1, 512), f32), V_((2, 8, D), f32),
             V_((128, D), f32), V_((2, 8, 64, D), f32), V_((2, 8, 64, D), bf16),
             V_((2, 8, 64, D), bf16), V_((4, 8, 64, D), bf16), V_((4, 8, 64, D), bf16),
-            dma((NC,)), dma((NC,)), dma, dma, dma((2, 2)), dma((2, 2)), dma((4, 16)), dma((4, 16)),
-            dma((4, 16)), dma((4, 16)),
-            dma, dma, dma((NC,)), dma((NC,)), dma((2, 2)), dma((2, 2)), dma((32,)), dma((32,)), dma, dma,
+            dma((16,)), dma((NC,)), dma((NC,)), dma((NC,)), dma((NC,)), dma((2, 2)), dma((2, 2)),
+            dma((4, 16)), dma((4, 16)), dma((4, 16)), dma((4, 16)),
+            dma((2,)), dma((2,)), dma((2, NC)), dma((2, NC)), dma((2, 2)), dma((2, 2)), dma((32,)), dma((32,)), dma, dma,
         ],
         compiler_params=pltpu.CompilerParams(
             collective_id=0, has_side_effects=True, vmem_limit_bytes=62 * 1024 * 1024
         ),
     )(
-        group_order, picture_starts, hidden_in.reshape(128, D), out_cotangent.reshape(128, D),
-        ws, proj_weight, down_weight,
-    )
-    me = NC * lax.axis_index("dp") + lax.axis_index("ctx")
-    grf = gr.astype(f32)
-    grad_qkv_weight = grf[:, :, :192].reshape(H, rows, 3, HD).transpose(1, 2, 0, 3).reshape(rows, 3 * D)
-    grad_up_weight = grf[:, :, 256:].transpose(1, 0, 2).reshape(rows, 4096)
-    gains = jnp.sum(grf[:, :, 192:196], axis=0)
-    tab = sr.reshape(2, 8, 2, 512).transpose(2, 1, 0, 3).reshape(H, 2, 512)
-    tsum = jnp.sum(tab, axis=1)
-    qkv_b = tsum[:, :192].reshape(H, 3, HD).transpose(1, 0, 2).reshape(3 * D)
-    up_b = tsum[:, 256:].reshape(4096)
-    head_max = jnp.max(tab[:, :, 192], axis=1)
-    grad_qkv_bias = lax.dynamic_slice(qkv_b, (96 * me,), (96,))
-    grad_up_bias = lax.dynamic_slice(up_b, (128 * me,), (128,))
-    grad_bias_out = lax.dynamic_slice(ds[0], (32 * me,), (32,))
-    clip_ratio = jnp.sqrt(clip_bound / jnp.maximum(head_max, clip_bound))
-    head_cols = jnp.repeat(clip_ratio, HD)
-    factor = jnp.concatenate([head_cols, head_cols, jnp.ones((D,), f32)])
-    clipped_qkv = qkv_weight.astype(f32) * factor[None, :]
-    return (
-        bo.reshape(2, 64, D), gh.reshape(2, 64, D), gains[:, 0], gains[:, 1],
-        grad_qkv_weight, grad_qkv_bias, gp[:32], grad_bias_out, gains[:, 2], gains[:, 3],
-        grad_up_weight, grad_up_bias, gp[32:], grad_bias_out, clipped_qkv,
-    )
+        group_order, picture_starts, hidden_in, out_cotangent, qkv_weight, up_weight, proj_weight, down_weight,
+        *(v.reshape(1, -1) for v in (
+            attn_gain, attn_shift, mlp_gain, mlp_shift, proj_bias, down_bias, qkv_bias, up_bias)),
+    )
+    r32 = sds((1, 32))
+    outs = pl.pallas_call(
+        finish_kernel,
+        out_shape=(
+            sds((2, 64, D), bf16), sds((2, 64, D), bf16), r32, r32, sds((32, 3 * D)), sds((1, 96)),
+            sds((32, D)), r32, r32, r32, sds((32, 4 * D)), sds((1, 128)), sds((128, D)), r32, sds((32, 3 * D)),
+        ),
+        in_specs=[vm] * 8,
+        out_specs=(vm,) * 15,
+        scratch_shapes=[V_((H, 512), f32), V_((64, 128), f32)],
+    )(*got, qkv_weight)
+    return tuple(o.reshape(-1) if o.shape[0] == 1 else o for o in outs)
 
 
 def solution(mesh):

time: 181 us -> 139 us (0.77)
  Pallas kernels: 157 us -> 137 us
  local copies, waits for them, and re-layouts: 18.5 us -> 0 us
  other arithmetic: 3.29 us -> 0 us
    pallas_call x1 -> x2, Pallas kernels: 157 us -> 137 us  [the longest x1 134 us: fast_shards(): pl.pallas_call(block_kernel, out_shape=(sds((128, D), bf16), sds((128, D)...]
    unnamed x36 -> x0, local copies, waits for them, and re-layouts: 8.55 us -> none
    reshape x14 -> x0, local copies, waits for them, and re-layouts: 4.45 us -> none  [the longest x3 1.79 us: fast_shards(): qkv_weight.reshape(rows, 3, H, HD).transpose(2, 0, 1, 3)]
    slice x6 -> x0, local copies, waits for them, and re-layouts: 3.03 us -> none  [the longest x1 0.83 us: fast_shards(): gp[32:]]
where the time goes in v2:
time: 139 us; the launch traced here: 138 us
  Pallas kernels  137 us (99%)
    pallas_call x1, Pallas kernels, fast_shards(): pl.pallas_call(block_kernel, out_shape=(sds((128, D), bf16), sds((128, D)...  134 us
    pallas_call x1, Pallas kernels, fast_shards(): pl.pallas_call(finish_kernel, out_shape=(sds((2, 64, D), bf16), sds((2, 6...  3.2 us

profile of v2, /device:TPU:0, one launch (start us, length us, event | category | flops | bytes accessed | tf_op | source)
XLA Modules:
  0.0 138.2 jit_solution(15994520307307432849)
XLA Ops:
  0.7 134.2 %shard_map.271 = (bf16[128,1024]{1,0:T(8,128)(2,1)}, bf16[128,1024]{1,0:T(8,128)(2,1)}, bf16[16,32,256]{2,1,0:T(8,128)(2,1)}, bf16[16,32,256]{2,1,0:T(8,128)(2,1...) custom-call(s32[16]{0:T(128)} %go_ref.1, s32[2,4]{1,0:T(2,128)} %ps_ref.1, ...), custom_call_target="tpu_custom_call" | custom-call | tf_op jit(solution)/shard_map/pallas_call | solution.py:1224
  134.9 3.2 %shard_map.272 = (bf16[2,64,1024]{2,1,0:T(8,128)(2,1)}, bf16[2,64,1024]{2,1,0:T(8,128)(2,1)}, f32[1,32]{1,0:T(1,128)}, f32[1,32]{1,0:T(1,128)}, f32[32,3072]{1,0...) custom-call(bf16[128,1024]{1,0:T(8,128)(2,1)} %get-tuple-element.37., ...), custom_call_target="tpu_custom_call" | custom-call | tf_op jit(solution)/shard_map/pallas_call | solution.py:1262

commit v3 on v2

--- a/solution.py
+++ b/solution.py
@@ -434,7 +434,7 @@
     QW, UW, V0, V1, V2, V3, V4, V5, V6, V7, WS,
     X, Y, NA, NM, WC, WPD, CT, ST, PK, LIM, SM, BV,
     Q, K, V, VT, KT, PT, ATT, AA, GP, DA, GG, DQ, DK, DV, HM, GN,
-    TT, GA, GB, GYA, GYB, GSA, GSB, PDS, PDR, SROW, DSUM,
+    TT, GA, GB, GYA, GYB, PDS, SROW, DSUM,
     TMP, LP, SB, RSB, SR, RR,
     in_s, w_s, w_r, wy_s, wy_r, pd_s, pd_r, ga_s, ga_r, rs_s, rs_r,
     gy_s, gy_r, gg_s, gg_r, gpd_s, gpd_r, sm_s, sm_r, dm_s, dm_r,
@@ -484,6 +484,58 @@
     fetch_y = [pltpu.make_async_copy(dy_ref.at[s], Y.at[own_rows(s)], in_s.at[12 + s]) for s in range(2)]
     for cp in fetch + fetch_x + fetch_y:
         cp.start()
+    pl.semaphore_wait(barrier, 31)
+
+    class Gather:
+        def __init__(self, buf, own, s, i):
+            self.buf, self.own, self.s, self.i = buf, own, s, i
+
+        def at(self, delta, core):
+            row = self.s * SL + 64 * ctx_of(r + delta, core)
+            return self.buf.at[pl.ds(pl.multiple_of(row, 64), 64)]
+
+        def ring(self, t, way, back=0):
+            region = self.at((t + back) * (2 * way - 1), j)
+            slot = 4 * way + t
+            return rcopy(region, region, ga_s.at[self.i, slot], ga_r.at[self.i, slot],
+                         left if way else right)
+
+        def steps(self, way):
+            return 4 if way == self.s else 3
+
+        def sib(self, slot, core):
+            delta = (0, -1, -2, -3, 1, 2, 3, 4)[slot]
+            region = self.at(delta, core)
+            return rcopy(region, region, ga_s.at[self.i, 8 + slot], ga_r.at[self.i, 8 + slot], sibling)
+
+        def start(self):
+            self.own[self.s].wait()
+            self.ring(0, 0).start()
+            self.ring(0, 1).start()
+            self.sib(0, j).start()
+
+        def pump(self, t):
+            for way in (0, 1):
+                if t <= self.steps(way):
+                    self.ring(t - 1, way, 1).wait_recv()
+                    if t < self.steps(way):
+                        self.ring(t, way).start()
+                    self.sib(7 if t == 4 else t + 3 * way, j).start()
+
+        def ready(self, t):
+            for slot in ((0,) if t == 0 else (t, 3 + t) if t < 4 else (7,)):
+                self.sib(slot, 1 - j).wait_recv()
+
+        def drain(self):
+            for way in (0, 1):
+                for t in range(self.steps(way)):
+                    self.ring(t, way).wait_send()
+            for slot in range(8):
+                self.sib(slot, j).wait_send()
+
+    gx = [Gather(X, fetch_x, s, s) for s in range(2)]
+    gd = [Gather(Y, fetch_y, s, 2 + s) for s in range(2)]
+    gx[0].start()
     for cp in fetch:
         cp.wait()
 
@@ -512,8 +564,6 @@
     for h in range(H):
         WS[h, :, 256:512] = UW[:, 256 * h:256 * h + 256]
 
-    pl.semaphore_wait(barrier, 31)
-
     def w_copy(o, dst_c, row):
         return rcopy(
             WS.at[8 * (dst_c % 2) + dst_c // 2],
@@ -536,63 +586,6 @@
         return rcopy(region, region, wy_s.at[o], wy_r.at[o], partner)
 
     wy_copy(0, d).start()
-
-    class Gather:
-        def __init__(self, buf, own, s, i):
-            self.buf, self.own, self.s, self.i = buf, own, s, i
-
-        def at(self, delta, core, lo=0, n=64):
-            row = self.s * SL + 64 * ctx_of(r + delta, core) + lo
-            return self.buf.at[pl.ds(pl.multiple_of(row, 32), n)]
-
-        def ring(self, t, way):
-            delta = -t if way == 0 else t
-            region = self.at(delta, j) if t < 3 else self.at(delta, j, 32 * way, 32)
-            slot = 4 * way + t
-            return rcopy(region, region, ga_s.at[self.i, slot], ga_r.at[self.i, slot],
-                         right if way == 0 else left)
-
-        def arrival(self, t, way):
-            delta = -(t + 1) if way == 0 else t + 1
-            region = self.at(delta, j) if t < 3 else self.at(delta, j, 32 * way, 32)
-            slot = 4 * way + t
-            return rcopy(region, region, ga_s.at[self.i, slot], ga_r.at[self.i, slot],
-                         right if way == 0 else left)
-
-        def sib(self, slot, core):
-            delta = (0, -1, -2, -3, 1, 2, 3, 4)[slot]
-            region = self.at(delta, core)
-            return rcopy(region, region, ga_s.at[self.i, 8 + slot], ga_r.at[self.i, 8 + slot], sibling)
-
-        def start(self):
-            self.own[self.s].wait()
-            self.ring(0, 0).start()
-            self.ring(0, 1).start()
-            self.sib(0, j).start()
-
-        def pump(self, t):
-            for way in (0, 1):
-                self.arrival(t - 1, way).wait_recv()
-                if t < 4:
-                    self.ring(t, way).start()
-                    self.sib((t if way == 0 else 3 + t), j).start()
-            if t == 4:
-                self.sib(7, j).start()
-
-        def ready(self, t):
-            for slot in ((0,) if t == 0 else (t, 3 + t) if t < 4 else (7,)):
-                self.sib(slot, 1 - j).wait_recv()
-
-        def drain(self):
-            for t in range(4):
-                self.ring(t, 0).wait_send()
-                self.ring(t, 1).wait_send()
-            for slot in range(8):
-                self.sib(slot, j).wait_send()
-
-    gx = [Gather(X, fetch_x, s, s) for s in range(2)]
-    gd = [Gather(Y, fetch_y, s, 2 + s) for s in range(2)]
-    gx[0].start()
     gx[1].start()
 
     def pd_copies(jj, dst_dp):
@@ -667,7 +660,6 @@
     lax.fori_loop(1, NC, w_wait, 0)
     pd_start()
     gx[0].pump(1)
-    gx[1].pump(1)
 
     def wy_wait(o, _):
         wy_copy(o, 1 - d).wait_recv()
@@ -703,9 +695,6 @@
     BV[0] = jnp.broadcast_to(bq, (8, 256))
     BV[1] = jnp.broadcast_to(bu, (8, 256))
 
-    ln128 = lane((128, 128))
-    low_half = ln128 < 64
-
     def turn(v, cs, sn, sign):
         l64 = lane(v.shape) & 63
         mate = jnp.where(l64 < ROT // 2, pltpu.roll(v, 120, 1), pltpu.roll(v, 8, 1))
@@ -717,65 +706,48 @@
         inv = lax.rsqrt(jnp.mean(cen * cen, axis=1, keepdims=True) + norm_eps)
         return cen * inv, inv
 
-    def n_stage(i, _):
-        rows = pl.ds(pl.multiple_of(i * 128, 128), 128)
-        trow = pl.ds(pl.multiple_of((i % 8) * 128, 128), 128)
-        nrm, _ = normed_of(X[rows, :])
+    def chip_rows(s, deltas):
+        return [pl.ds(pl.multiple_of(s * SL + 64 * ctx_of(r + e, 0), 128), 128) for e in deltas]
+
+    def load(ref, rows, lo=0, hi=None):
+        parts = [ref[x, lo:hi] for x in rows]
+        return parts[0] if len(parts) == 1 else jnp.concatenate(parts, axis=0)
+
+    def store(ref, rows, value, lo=0, hi=None):
+        for i, x in enumerate(rows):
+            ref[x, lo:hi] = value[128 * i:128 * i + 128]
+
+    def n_stage(s, deltas):
+        rows, trow = chip_rows(s, deltas), chip_rows(0, deltas)
+        low = lane((128 * len(rows), 128)) < 64
+        nrm, _ = normed_of(load(X, rows))
         na = (nrm * SM[0:1, :] + SM[1:2, :]).astype(bf16)
         nm = (nrm * SM[2:3, :] + SM[3:4, :]).astype(bf16)
-        NA[rows, :] = na
-        NM[rows, :] = nm
+        store(NA, rows, na)
+        store(NM, rows, nm)
         qkv = dot(na, WC[:, 0:256]) + BV[0, 0:1, :]
         up = dot(nm, WC[:, 256:512]) + BV[1, 0:1, :]
-        rot = turn(qkv[:, 0:128], CT[trow, :], ST[trow, :], 1.0)
-        Q[rows, :] = jnp.where(low_half, rot * 0.125, 0.0).astype(bf16)
-        K[rows, :] = jnp.where(low_half, pltpu.roll(rot, 64, 1), 0.0).astype(bf16)
-        V[rows, :] = jnp.where(low_half, qkv[:, 128:256], 0.0).astype(bf16)
+        rot = turn(qkv[:, 0:128], load(CT, trow), load(ST, trow), 1.0)
+        store(Q, rows, jnp.where(low, rot * 0.125, 0.0).astype(bf16))
+        store(K, rows, jnp.where(low, pltpu.roll(rot, 64, 1), 0.0).astype(bf16))
+        store(V, rows, jnp.where(low, qkv[:, 128:256], 0.0).astype(bf16))
         cdf = 0.5 * (1.0 + lax.erf(up * (2.0 ** -0.5)))
-        AA[rows, 0:256] = (up * cdf).astype(bf16)
-        GP[rows, :] = cdf + up * (jnp.exp(-0.5 * up * up) * ((2.0 * math.pi) ** -0.5))
-        return 0
-
-    def n_blocks(t):
-        for s in range(2):
-            gx[s].ready(t)
-        count = 2 if t in (0, 4) else 4
-
-        def one(i, _):
-            s = i % 2
-            delta = t * (1 - 2 * (i // 2))
-            return n_stage(8 * s + ctx_of(r + delta, 0) // 2, 0)
-
-        lax.fori_loop(0, count, one, 0)
+        store(AA, rows, (up * cdf).astype(bf16), 0, 256)
+        store(GP, rows, cdf + up * (jnp.exp(-0.5 * up * up) * ((2.0 * math.pi) ** -0.5)))
+
+    def n_blocks(s, t):
+        gx[s].ready(t)
+        n_stage(s, (t,) if t in (0, 4) else (t, -t))
 
     def dy_blocks(s, t):
+        if t == 0:
+            gd[s].ready(4)
         gd[s].ready(t)
-        count = 1 if t in (0, 4) else 2
-
-        def one(i, _):
-            return dy_stage(8 * s + ctx_of(r + t * (1 - 2 * i), 0) // 2, 0)
-
-        lax.fori_loop(0, count, one, 0)
-
-    n_blocks(0)
-    gx[0].pump(2)
-    gx[1].pump(2)
-    n_blocks(1)
-    gd[0].start()
-    gx[0].pump(3)
-    gx[1].pump(3)
-    n_blocks(2)
-    gd[1].start()
-    gx[0].pump(4)
-    gx[1].pump(4)
-    n_blocks(3)
-    gd[0].pump(1)
-    n_blocks(4)
-    gd[1].pump(1)
-
-    for s in range(2):
-        VT[s] = V[s * SL:s * SL + SL, :].astype(f32).T.astype(bf16)
-        KT[s] = K[s * SL:s * SL + SL, :].astype(f32).T.astype(bf16)
+        dy_stage(s, (0, 4) if t == 0 else (t, -t))
+
+    def turn_kv(s):
+        VT[s] = V[s * SL:s * SL + SL, :].astype(f32).T[0:64, :].astype(bf16)
+        KT[s] = K[s * SL:s * SL + SL, :].astype(f32).T[0:64, :].astype(bf16)
 
     HM[...] = jnp.full((8, 256), masked_score, f32)
 
@@ -795,61 +767,43 @@
         PT[i] = pt
         at = dot(VT[s], pt)
         ATT[i] = at
-        AA[rows, 256:384] = at.T.astype(bf16)
+        AA[rows, 256:384] = jnp.concatenate([at, jnp.zeros((64, 256), f32)], axis=0).T.astype(bf16)
         HM[...] = jnp.maximum(HM[...], jnp.broadcast_to(peak, (8, 256)))
         return 0
 
     class Scatter:
-        def __init__(self, i, s, partial):
-            self.i, self.s, self.partial = i, s, partial
+        def __init__(self, i, s, group, partial):
+            self.i, self.s, self.g, self.partial = i, s, group, partial
 
         def sib(self, slot):
-            return rcopy(SB.at[self.s, slot], SR.at[self.i, slot],
+            return rcopy(SB.at[self.g, slot], SR.at[self.i, slot],
                          rs_s.at[self.i, 8 + slot], rs_r.at[self.i, 8 + slot], sibling)
 
-        def produce(self):
-            def one(slot, _):
-                mag = 3 - (slot + 1) // 2 + 1
-                delta = mag * (2 * (slot % 2) - 1)
-                row = self.s * SL + 64 * ctx_of(r + delta, 0)
-                TMP[...] = self.partial(row)
-                LP[self.s, slot] = TMP[pl.ds(pl.multiple_of(64 * j, 64), 64), :]
-                SB[self.s, slot] = TMP[pl.ds(pl.multiple_of(64 * (1 - j), 64), 64), :].astype(bf16)
+        def produce(self, p):
+            value = self.partial(self.s, (4, 0) if p == 0 else (4 - p, p - 4))
+            for i, slot in enumerate((0, 7) if p == 0 else (2 * p - 1, 2 * p)):
+                TMP[...] = value[128 * i:128 * i + 128]
+                LP[self.g, slot] = TMP[pl.ds(pl.multiple_of(64 * j, 64), 64), :]
+                SB[self.g, slot] = TMP[pl.ds(pl.multiple_of(64 * (1 - j), 64), 64), :].astype(bf16)
                 self.sib(slot).start()
-                return 0
-            lax.fori_loop(0, 8, one, 0)
 
         def lane_sum(self, slot):
             self.sib(slot).wait_recv()
-            return LP[self.s, slot] + SR[self.i, slot].astype(f32)
+            return LP[self.g, slot] + SR[self.i, slot].astype(f32)
 
         def ring(self, t, way):
             slot = 4 * way + t
-            n = 32 if t == 0 else 64
-            return rcopy(RSB.at[self.s, slot, pl.ds(0, n)], RR.at[self.i, slot, pl.ds(0, n)],
-                         rs_s.at[self.i, slot], rs_r.at[self.i, slot], right if way == 0 else left)
+            return rcopy(RSB.at[self.g, slot], RR.at[self.i, slot],
+                         rs_s.at[self.i, slot], rs_r.at[self.i, slot], left if way else right)
 
         def pump(self, t):
-            if t == 0:
-                v = self.lane_sum(0)
-                for way in (0, 1):
-                    RSB[self.s, 4 * way, 0:32, :] = v[32 * way:32 * way + 32].astype(bf16)
-                    self.ring(0, way).start()
-                return
-            for way in (0, 1):
-                v = self.lane_sum(2 * t - 1 + way)
-                self.ring(t - 1, way).wait_recv()
+            for way in (self.s,) if t == 0 else (0, 1):
                 slot = 4 * way + t
-                if t == 1:
-                    got = RR[self.i, 4 * way, 0:32, :].astype(f32)
-                    if way == 0:
-                        RSB[self.s, slot, 0:32, :] = (v[0:32] + got).astype(bf16)
-                        RSB[self.s, slot, 32:64, :] = v[32:64].astype(bf16)
-                    else:
-                        RSB[self.s, slot, 0:32, :] = v[0:32].astype(bf16)
-                        RSB[self.s, slot, 32:64, :] = (v[32:64] + got).astype(bf16)
-                else:
-                    RSB[self.s, slot] = (v + RR[self.i, slot - 1].astype(f32)).astype(bf16)
+                v = self.lane_sum(2 * t - 1 + way if t else 0)
+                if t > 1 or (t == 1 and way == self.s):
+                    self.ring(t - 1, way).wait_recv()
+                    v = v + RR[self.i, slot - 1].astype(f32)
+                RSB[self.g, slot] = v.astype(bf16)
                 self.ring(t, way).start()
 
         def total(self):
@@ -862,24 +816,23 @@
         def drain(self):
             for slot in range(8):
                 self.sib(slot).wait_send()
-            for t in range(4):
-                self.ring(t, 0).wait_send()
-                self.ring(t, 1).wait_send()
-
-    def out_partial(row):
-        return dot(AA[pl.ds(pl.multiple_of(row, 128), 128), :], WPD[...])
-
-    out = [Scatter(s, s, out_partial) for s in range(2)]
+            for way in (0, 1):
+                for t in range(0 if way == self.s else 1, 4):
+                    self.ring(t, way).wait_send()
+
+    def out_partial(s, deltas):
+        return dot(load(AA, chip_rows(s, deltas)), WPD[...])
+
+    out = [Scatter(s, s, s, out_partial) for s in range(2)]
     DSUM[d] = jnp.zeros((8, D), f32)
 
-    def dy_stage(i, _):
-        rows = pl.ds(pl.multiple_of(i * 128, 128), 128)
-        dyb = Y[rows, :]
+    def dy_stage(s, deltas):
+        rows = chip_rows(s, deltas)
+        dyb = load(Y, rows)
         back = dot_nt(dyb, WPD[...])
-        GG[rows, 256:512] = (back[:, 0:256] * GP[rows, :]).astype(bf16)
-        DA[rows, :] = back[:, 256:384].astype(bf16)
+        store(GG, rows, (back[:, 0:256] * load(GP, rows)).astype(bf16), 256, 512)
+        store(DA, rows, back[:, 256:384].astype(bf16))
         DSUM[d] += jnp.broadcast_to(jnp.sum(dyb.astype(f32), axis=0, keepdims=True), (8, D))
-        return 0
 
     def bwd(i, _):
         s = i // 4
@@ -887,13 +840,13 @@
         seq = pl.ds(pl.multiple_of(s * SL, SL), SL)
         q0 = pl.ds(pl.multiple_of((i % 4) * 256, 256), 256)
         da = DA[rows, :]
-        rd = jnp.sum(da.astype(f32).T * ATT[i], axis=0, keepdims=True)
+        rd = jnp.sum(da.astype(f32).T[0:64, :] * ATT[i], axis=0, keepdims=True)
         dpt = dot_nt(V[seq, :], da)
         pt = PT[i]
         ds = (pt.astype(f32) * (dpt - rd)).astype(bf16)
         DV[...] += dot(pt, da)
         DK[...] += dot(ds, Q[rows, :])
-        DQ[q0, :] = dot(KT[s], ds).T * 0.125
+        DQ[q0, :] = jnp.concatenate([dot(KT[s], ds), jnp.zeros((64, 256), f32)], axis=0).T * 0.125
         return 0
 
     def qkv_back(i, s):
@@ -906,18 +859,18 @@
 
     GN[...] = jnp.zeros((8, D), f32)
 
-    def g_partial(row):
-        rows = pl.ds(pl.multiple_of(row, 128), 128)
-        nrm, _ = normed_of(X[rows, :])
-        gna = dot_nt(GG[rows, 0:256], WC[:, 0:256])
-        gnm = dot_nt(GG[rows, 256:512], WC[:, 256:512])
+    def g_partial(s, deltas):
+        rows = chip_rows(s, deltas)
+        nrm, _ = normed_of(load(X, rows))
+        gna = dot_nt(load(GG, rows, 0, 256), WC[:, 0:256])
+        gnm = dot_nt(load(GG, rows, 256, 512), WC[:, 256:512])
         GN[0:1, :] += jnp.sum(gna * nrm, axis=0, keepdims=True)
         GN[1:2, :] += jnp.sum(gna, axis=0, keepdims=True)
         GN[2:3, :] += jnp.sum(gnm * nrm, axis=0, keepdims=True)
         GN[3:4, :] += jnp.sum(gnm, axis=0, keepdims=True)
         return gna * SM[0:1, :] + gnm * SM[2:3, :]
 
-    grad = [Scatter(2 + s, s, g_partial) for s in range(2)]
+    grad = [Scatter(2 + s, s, s, g_partial) for s in range(2)]
 
     def out_done(s):
         tot = out[s].total()
@@ -930,66 +883,12 @@
         DV[...] = jnp.zeros((SL, 128), f32)
         DK[...] = jnp.zeros((SL, 128), f32)
 
-    gd[0].pump(2)
-    lax.fori_loop(0, 2, fwd, 0)
-    for jj in range(2):
-        @pl.when(jnp.logical_not(here & (j == jj)))
-        def _():
-            for cp in pd_copies(jj, 0):
-                cp.wait_recv()
-
-    @pl.when(here)
-    def _():
-        for cp in local_pd:
-            cp.wait()
-
-    gd[1].pump(2)
-    lax.fori_loop(2, 4, fwd, 0)
-    gd[0].pump(3)
-    out[0].produce()
-    out[0].pump(0)
-    gd[1].pump(3)
-    lax.fori_loop(4, 6, fwd, 0)
-    gd[0].pump(4)
-    out[0].pump(1)
-    lax.fori_loop(6, 8, fwd, 0)
-    gd[1].pump(4)
-    out[1].produce()
-    out[1].pump(0)
-    out[0].pump(2)
-    for t in range(5):
-        dy_blocks(0, t)
-    out[1].pump(1)
-    for t in range(5):
-        dy_blocks(1, t)
-    dm = rcopy(DSUM.at[d], DSUM.at[d], dm_s, dm_r, partner)
-    dm.start()
-    out[0].pump(3)
-    out[1].pump(2)
-    bwd_start()
-    lax.fori_loop(0, 4, bwd, 0)
-    lax.fori_loop(0, 8, qkv_back, 0)
-    out[1].pump(3)
-    out_done(0)
-    grad[0].produce()
-    grad[0].pump(0)
-    bwd_start()
-    lax.fori_loop(4, 6, bwd, 0)
-    grad[0].pump(1)
-    out_done(1)
-    lax.fori_loop(6, 8, bwd, 0)
-    grad[0].pump(2)
-    lax.fori_loop(0, 8, qkv_back, 1)
-    grad[1].produce()
-    grad[1].pump(0)
-    grad[0].pump(3)
-
-    def transpose_gg(i, _):
-        rows = pl.ds(pl.multiple_of(i * 256, 256), 256)
-        TT[:, rows] = GG[rows, :].T
-        return 0
-
-    lax.fori_loop(0, 8, transpose_gg, 0)
+    def transpose_gg(lo):
+        def one(i, _):
+            rows = pl.ds(pl.multiple_of(i * 256, 256), 256)
+            TT[0:256, rows] = GG[rows, lo:lo + 256].T
+            return 0
+        lax.fori_loop(0, 8, one, 0)
 
     def qkv_grad(i, _):
         cols = pl.ds(pl.multiple_of(i * 256, 256), 256)
@@ -1000,89 +899,113 @@
 
     def up_grad(i, _):
         cols = pl.ds(pl.multiple_of(i * 256, 256), 256)
-        GB[cols, :] = dot(TT[256:512, :], NM[:, cols]).T.astype(bf16)
-        return 0
-
-    lax.fori_loop(0, 4, qkv_grad, 0)
+        GB[cols, :] = dot(TT[0:256, :], NM[:, cols]).T.astype(bf16)
+        return 0
+
     gya = rcopy(GA.at[other], GYA, gy_s.at[0], gy_r.at[0], partner)
-    gya.start()
-    grad[1].pump(1)
-    lax.fori_loop(0, 4, up_grad, 0)
     gyb = rcopy(GB.at[other], GYB, gy_s.at[1], gy_r.at[1], partner)
-    gyb.start()
+
+    def up_weights():
+        transpose_gg(256)
+        lax.fori_loop(0, 4, up_grad, 0)
+        gyb.start()
+
+    def qkv_weights():
+        transpose_gg(0)
+        lax.fori_loop(0, 4, qkv_grad, 0)
+        gya.start()
 
     def transpose_aa(i, _):
         rows = pl.ds(pl.multiple_of(i * 256, 256), 256)
-        TT[0:384, rows] = AA[rows, :].T
-        return 0
-
-    lax.fori_loop(0, 8, transpose_aa, 0)
+        TT[:, rows] = AA[rows, :].T
+        return 0
 
     def pd_grad(i, _):
         cols = pl.ds(pl.multiple_of(i * 256, 256), 256)
-        PDS[:, cols] = dot(TT[0:384, :], Y[:, cols]).astype(bf16)
-        return 0
-
-    lax.fori_loop(0, 4, pd_grad, 0)
+        PDS[:, cols] = dot(TT[...], Y[:, cols]).astype(bf16)
+        return 0
 
     def gpd_copies(jj, slot_dp):
         dev = (j, 2 * k + jj)
         return (
-            rcopy(PDS.at[pl.ds(256 + 32 * jj, 32)], PDR.at[slot_dp, pl.ds(0, 32)],
+            rcopy(PDS.at[pl.ds(256 + 32 * jj, 32)], gp_ref.at[slot_dp, pl.ds(0, 32)],
                   gpd_s.at[jj, 0], gpd_r.at[slot_dp, 0], dev),
-            rcopy(PDS.at[pl.ds(128 * jj, 128)], PDR.at[slot_dp, pl.ds(32, 128)],
+            rcopy(PDS.at[pl.ds(128 * jj, 128)], gp_ref.at[slot_dp, pl.ds(32, 128)],
                   gpd_s.at[jj, 1], gpd_r.at[slot_dp, 1], dev),
         )
 
-    for jj in range(2):
-        @pl.when(jnp.logical_not(here & (j == jj)))
+    def pd_weights():
+        lax.fori_loop(0, 8, transpose_aa, 0)
+        lax.fori_loop(0, 4, pd_grad, 0)
+        for jj in range(2):
+            @pl.when(jnp.logical_not(here & (j == jj)))
+            def _():
+                for cp in gpd_copies(jj, d):
+                    cp.start()
+
+        @pl.when(here)
         def _():
-            for cp in gpd_copies(jj, d):
-                cp.start()
-
-    @pl.when(here)
-    def _():
-        PDR[d, 0:32, :] = PDS[pl.ds(256 + 32 * j, 32), :]
-        PDR[d, 32:160, :] = PDS[pl.ds(128 * j, 128), :]
-
-    grad[1].pump(2)
-
-    srow = jnp.zeros((1, 512), f32)
-    for i in range(TOK // 256):
-        srow = srow + jnp.sum(GG[i * 256:i * 256 + 256, :].astype(f32), axis=0, keepdims=True)
-    hmax = jnp.max(HM[...], axis=1, keepdims=True)[0:1, :]
-    SROW[...] = jnp.where(lane((1, 512)) == 192, hmax, srow)
+            gp_ref[d, 0:32, :] = PDS[pl.ds(256 + 32 * j, 32), :]
+            gp_ref[d, 32:160, :] = PDS[pl.ds(128 * j, 128), :]
+
+    def g_copy(half_i, o, dst_c, slot):
+        src, dst = ((GA, gra_ref), (GB, grb_ref))[half_i]
+        return rcopy(src.at[pl.ds(pl.multiple_of(512 * d + 32 * dst_c, 32), 32)], dst.at[slot],
+                     gg_s.at[half_i, o], gg_r.at[half_i, o], (d, dst_c))
+
+    def weights_out(half_i):
+        gy, G, GY, gr_ref = ((gya, GA, GYA, gra_ref), (gyb, GB, GYB, grb_ref))[half_i]
+        gy.wait_recv()
+        G[half, :] = (G[half, :].astype(f32) + GY[...].astype(f32)).astype(bf16)
+
+        def g_send(o, _):
+            g_copy(half_i, o, (c + o) % NC, head).start()
+            return 0
+
+        lax.fori_loop(1, NC, g_send, 0)
+        gr_ref[head] = G[pl.ds(pl.multiple_of(512 * d + 32 * c, 32), 32), :]
+
+    def pd_ready():
+        for jj in range(2):
+            @pl.when(jnp.logical_not(here & (j == jj)))
+            def _():
+                for cp in pd_copies(jj, 0):
+                    cp.wait_recv()
+
+        @pl.when(here)
+        def _():
+            for cp in local_pd:
+                cp.wait()
+
+    def fwd_tiles(lo, hi):
+        lax.fori_loop(lo, hi, fwd, 0)
+
+    def bwd_tiles(lo, hi):
+        lax.fori_loop(lo, hi, bwd, 0)
+
+    dm = rcopy(DSUM.at[d], DSUM.at[d], dm_s, dm_r, partner)
+
     me = NC * d + c
-    sr_ref[me] = SROW[...]
 
     def s_copy(o, slot):
         lin = (me + o) % 32
         return rcopy(SROW, sr_ref.at[slot], sm_s.at[o], sm_r.at[o], (lin // NC, lin % NC))
 
-    def s_send(o, _):
-        s_copy(o, me).start()
-        return 0
-
-    lax.fori_loop(1, 32, s_send, 0)
-
-    def g_copy(half_i, o, dst_c, slot):
-        src, dst = ((GSA, gra_ref), (GSB, grb_ref))[half_i]
-        return rcopy(src.at[pl.ds(pl.multiple_of(32 * dst_c, 32), 32)], dst.at[slot],
-                     gg_s.at[half_i, o], gg_r.at[half_i, o], (d, dst_c))
-
-    for half_i, (gy, G, GY, GS, gr_ref) in enumerate(((gya, GA, GYA, GSA, gra_ref), (gyb, GB, GYB, GSB, grb_ref))):
-        gy.wait_recv()
-        GS[...] = (G[half, :].astype(f32) + GY[...].astype(f32)).astype(bf16)
-
-        def g_send(o, _):
-            g_copy(half_i, o, (c + o) % NC, head).start()
+    def token_sums():
+        srow = jnp.zeros((1, 512), f32)
+        for i in range(TOK // 256):
+            srow = srow + jnp.sum(GG[i * 256:i * 256 + 256, :].astype(f32), axis=0, keepdims=True)
+        hmax = jnp.max(HM[...], axis=1, keepdims=True)[0:1, :]
+        SROW[...] = jnp.where(lane((1, 512)) == 192, hmax, srow)
+        sr_ref[me] = SROW[...]
+
+        def s_send(o, _):
+            s_copy(o, me).start()
             return 0
 
-        lax.fori_loop(1, NC, g_send, 0)
-        gr_ref[head] = GS[pl.ds(pl.multiple_of(32 * c, 32), 32), :]
-    grad[1].pump(3)
-
-    for s in range(2):
+        lax.fori_loop(1, 32, s_send, 0)
+
+    def grad_done(s):
         tot = grad[s].total()
         own = slice(s * 64, s * 64 + 64)
         nrm, inv = normed_of(X[own_rows(s), :])
@@ -1092,12 +1015,105 @@
                      - nrm * jnp.mean(tot * nrm, axis=1, keepdims=True))
         ).astype(bf16)
 
+    gx[1].pump(1)
+    gx[0].pump(2)
+    gx[1].pump(2)
+    n_blocks(0, 2)
+    n_blocks(1, 1)
+    gx[0].pump(3)
+    gd[0].start()
+    n_blocks(0, 0)
+    gx[1].pump(3)
+    n_blocks(0, 3)
+    gd[1].start()
+    n_blocks(0, 1)
+    n_blocks(1, 3)
+    gx[0].pump(4)
+    n_blocks(1, 2)
+    n_blocks(0, 4)
+    gd[0].pump(1)
+    n_blocks(1, 0)
+    turn_kv(0)
+    fwd_tiles(0, 2)
+    gd[1].pump(1)
+    fwd_tiles(2, 4)
+    pd_ready()
+    out[0].produce(0)
+    out[0].produce(1)
+    gx[1].pump(4)
+    out[0].produce(2)
+    gd[0].pump(2)
+    n_blocks(1, 4)
+    gd[1].pump(2)
+    dy_blocks(0, 2)
+    turn_kv(1)
+    out[0].pump(0)
+    out[0].produce(3)
+    fwd_tiles(4, 6)
+    gd[0].pump(3)
+    fwd_tiles(6, 8)
+    gd[1].pump(3)
+    dy_blocks(1, 1)
+    out[1].produce(0)
+    out[1].pump(0)
+    out[1].produce(1)
+    out[0].pump(1)
+    dy_blocks(0, 1)
+    out[1].produce(2)
+    dy_blocks(1, 2)
+    gd[1].pump(4)
+    dy_blocks(0, 3)
+    dy_blocks(1, 0)
+    gd[0].pump(4)
+    dy_blocks(1, 3)
+    dy_blocks(0, 0)
+    out[1].pump(1)
+    bwd_start()
+    up_weights()
+    out[0].pump(2)
+    bwd_tiles(0, 2)
+    out[1].pump(2)
+    out[1].produce(3)
+    bwd_tiles(2, 4)
+    lax.fori_loop(0, 8, qkv_back, 0)
+    out[0].pump(3)
+    dm.start()
+    bwd_start()
+    bwd_tiles(4, 6)
+    out[1].pump(3)
+    bwd_tiles(6, 8)
+    weights_out(1)
+    lax.fori_loop(0, 8, qkv_back, 1)
+    out_done(0)
+    out_done(1)
+    grad[1].produce(0)
+    grad[0].produce(0)
+    grad[1].pump(0)
+    grad[0].produce(1)
+    grad[0].pump(0)
+    grad[1].produce(1)
+    grad[0].produce(2)
+    grad[0].produce(3)
+    grad[1].pump(1)
+    grad[0].pump(1)
+    grad[1].produce(2)
+    grad[1].pump(2)
+    grad[1].produce(3)
+    qkv_weights()
+    grad[0].pump(2)
+    grad[1].pump(3)
+    pd_weights()
+    grad[0].pump(3)
+    weights_out(0)
+    grad_done(0)
+    token_sums()
+    grad_done(1)
+
     for e in range(2):
         @pl.when(jnp.logical_not(here & (d == e)))
         def _():
             for cp in gpd_copies(0, e):
                 cp.wait_recv()
-    gp_ref[...] = PDR[0].astype(f32) + PDR[1].astype(f32)
 
     rcopy(DSUM.at[1 - d], DSUM.at[1 - d], dm_s, dm_r, partner).wait_recv()
     ds_ref[...] = DSUM[0] + DSUM[1]
@@ -1157,8 +1173,8 @@
     for s in range(2):
         o_bo[s] = bo[64 * s:64 * s + 64, :]
         o_gh[s] = gh[64 * s:64 * s + 64, :]
-    o_pw[...] = gp[0:32, :]
-    o_dw[...] = gp[32:160, :]
+    o_pw[...] = gp[0, 0:32, :].astype(f32) + gp[1, 0:32, :].astype(f32)
+    o_dw[...] = gp[0, 32:160, :].astype(f32) + gp[1, 32:160, :].astype(f32)
     low = lax.broadcasted_iota(jnp.int32, (32, 128), 1) < 64
     low1 = low[0:1]
     gains = jnp.zeros((32, 128), f32)
@@ -1225,7 +1241,7 @@
         block_kernel,
         out_shape=(
             sds((128, D), bf16), sds((128, D), bf16), sds((NC, 32, 256), bf16), sds((NC, 32, 256), bf16),
-            sds((160, D)), sds((32, 1, 512)), sds((8, D)),
+            sds((2, 160, D), bf16), sds((32, 1, 512)), sds((8, D)),
         ),
         in_specs=[sm, sm] + [hbm] * 14,
         out_specs=(vm,) * 7,
@@ -1236,14 +1252,14 @@
             V_((SL, 128), f32), V_((SL, 128), f32), V_((SL, 128), jnp.int32),
             V_((2, 8, SL), jnp.int32), V_((16, D), f32), V_((2, 8, 256), f32),
             V_((TOK, 128), bf16), V_((TOK, 128), bf16), V_((TOK, 128), bf16),
-            V_((2, 128, SL), bf16), V_((2, 128, SL), bf16),
-            V_((8, SL, 256), bf16), V_((8, 128, 256), f32),
+            V_((2, 64, SL), bf16), V_((2, 64, SL), bf16),
+            V_((8, SL, 256), bf16), V_((8, 64, 256), f32),
             V_((TOK, 384), bf16), V_((TOK, 256), f32), V_((TOK, 128), bf16), V_((TOK, 512), bf16),
             V_((SL, 128), f32), V_((SL, 128), f32), V_((SL, 128), f32),
             V_((8, 256), f32), V_((8, D), f32),
-            V_((512, TOK), bf16), V_((D, 256), bf16), V_((D, 256), bf16),
-            V_((512, 256), bf16), V_((512, 256), bf16), V_((512, 256), bf16), V_((512, 256), bf16),
-            V_((384, D), bf16), V_((2, 160, D), bf16), V_((1, 512), f32), V_((2, 8, D), f32),
+            V_((384, TOK), bf16), V_((D, 256), bf16), V_((D, 256), bf16),
+            V_((512, 256), bf16), V_((512, 256), bf16),
+            V_((384, D), bf16), V_((1, 512), f32), V_((2, 8, D), f32),
             V_((128, D), f32), V_((2, 8, 64, D), f32), V_((2, 8, 64, D), bf16),
             V_((2, 8, 64, D), bf16), V_((4, 8, 64, D), bf16), V_((4, 8, 64, D), bf16),
             dma((16,)), dma((NC,)), dma((NC,)), dma((NC,)), dma((NC,)), dma((2, 2)), dma((2, 2)),
@@ -1251,7 +1267,7 @@
             dma((2,)), dma((2,)), dma((2, NC)), dma((2, NC)), dma((2, 2)), dma((2, 2)), dma((32,)), dma((32,)), dma, dma,
         ],
         compiler_params=pltpu.CompilerParams(
-            collective_id=0, has_side_effects=True, vmem_limit_bytes=62 * 1024 * 1024
+            collective_id=0, has_side_effects=True, vmem_limit_bytes=63 * 1024 * 1024
         ),
     )(
         group_order, picture_starts, hidden_in, out_cotangent, qkv_weight, up_weight, proj_weight, down_weight,

time: 139 us -> 132 us (0.950)
  Pallas kernels: 137 us -> 131 us
    pallas_call x1, Pallas kernels: 134 us -> 128 us  [fast_shards(): pl.pallas_call(block_kernel, out_shape=(sds((128, D), bf16), sds((128, D)...]
where the time goes in v3:
time: 132 us
  Pallas kernels  131 us (99%)
    pallas_call x1, Pallas kernels, fast_shards(): pl.pallas_call(block_kernel, out_shape=(sds((128, D), bf16), sds((128, D)...  128 us
    pallas_call x1, Pallas kernels, fast_shards(): pl.pallas_call(finish_kernel, out_shape=(sds((2, 64, D), bf16), sds((2, 6...  3.19 us

profile of v3, /device:TPU:0, one launch (start us, length us, event | category | flops | bytes accessed | tf_op | source)
XLA Modules:
  0.0 132.1 jit_solution(4150492228246260023)
XLA Ops:
  0.7 128.2 %shard_map.271 = (bf16[128,1024]{1,0:T(8,128)(2,1)}, bf16[128,1024]{1,0:T(8,128)(2,1)}, bf16[16,32,256]{2,1,0:T(8,128)(2,1)}, bf16[16,32,256]{2,1,0:T(8,128)(2,1...) custom-call(s32[16]{0:T(128)} %go_ref.1, s32[2,4]{1,0:T(2,128)} %ps_ref.1, ...), custom_call_target="tpu_custom_call" | custom-call | tf_op jit(solution)/shard_map/pallas_call | solution.py:1240
  128.9 3.2 %shard_map.272 = (bf16[2,64,1024]{2,1,0:T(8,128)(2,1)}, bf16[2,64,1024]{2,1,0:T(8,128)(2,1)}, f32[1,32]{1,0:T(1,128)}, f32[1,32]{1,0:T(1,128)}, f32[32,3072]{1,0...) custom-call(bf16[128,1024]{1,0:T(8,128)(2,1)} %get-tuple-element.37., ...), custom_call_target="tpu_custom_call" | custom-call | tf_op jit(solution)/shard_map/pallas_call | solution.py:1278

commit v4 on v3

--- a/solution.py
+++ b/solution.py
@@ -1017,97 +1017,97 @@
 
     gx[1].pump(1)
     gx[0].pump(2)
+    n_blocks(1, 0)
+    n_blocks(0, 1)
     gx[1].pump(2)
     n_blocks(0, 2)
     n_blocks(1, 1)
     gx[0].pump(3)
     gd[0].start()
     n_blocks(0, 0)
+    pd_ready()
+    n_blocks(0, 3)
     gx[1].pump(3)
-    n_blocks(0, 3)
-    gd[1].start()
-    n_blocks(0, 1)
     n_blocks(1, 3)
     gx[0].pump(4)
     n_blocks(1, 2)
+    gd[1].start()
     n_blocks(0, 4)
-    gd[0].pump(1)
-    n_blocks(1, 0)
     turn_kv(0)
     fwd_tiles(0, 2)
+    gd[0].pump(1)
+    gx[1].pump(4)
+    fwd_tiles(2, 4)
     gd[1].pump(1)
-    fwd_tiles(2, 4)
-    pd_ready()
+    n_blocks(1, 4)
+    turn_kv(1)
+    fwd_tiles(4, 6)
+    gd[0].pump(2)
+    fwd_tiles(6, 8)
     out[0].produce(0)
     out[0].produce(1)
-    gx[1].pump(4)
+    dy_blocks(1, 1)
+    gd[1].pump(2)
     out[0].produce(2)
-    gd[0].pump(2)
-    n_blocks(1, 4)
-    gd[1].pump(2)
+    out[0].produce(3)
+    out[1].produce(0)
+    out[0].pump(0)
+    dy_blocks(0, 1)
+    out[1].produce(1)
+    out[1].pump(0)
+    gd[0].pump(3)
+    out[1].produce(2)
+    out[1].produce(3)
+    gd[1].pump(3)
     dy_blocks(0, 2)
-    turn_kv(1)
-    out[0].pump(0)
-    out[0].produce(3)
-    fwd_tiles(4, 6)
-    gd[0].pump(3)
-    fwd_tiles(6, 8)
-    gd[1].pump(3)
-    dy_blocks(1, 1)
-    out[1].produce(0)
-    out[1].pump(0)
-    out[1].produce(1)
     out[0].pump(1)
-    dy_blocks(0, 1)
-    out[1].produce(2)
+    out[1].pump(1)
     dy_blocks(1, 2)
     gd[1].pump(4)
+    gd[0].pump(4)
+    dy_blocks(1, 0)
+    dy_blocks(0, 0)
+    dy_blocks(1, 3)
     dy_blocks(0, 3)
-    dy_blocks(1, 0)
-    gd[0].pump(4)
-    dy_blocks(1, 3)
-    dy_blocks(0, 0)
-    out[1].pump(1)
     bwd_start()
+    out[0].pump(2)
     up_weights()
-    out[0].pump(2)
+    out[1].pump(2)
     bwd_tiles(0, 2)
-    out[1].pump(2)
-    out[1].produce(3)
     bwd_tiles(2, 4)
+    out[0].pump(3)
     lax.fori_loop(0, 8, qkv_back, 0)
-    out[0].pump(3)
-    dm.start()
+    out[1].pump(3)
     bwd_start()
     bwd_tiles(4, 6)
-    out[1].pump(3)
     bwd_tiles(6, 8)
     weights_out(1)
+    out_done(0)
+    grad[0].produce(0)
+    grad[0].produce(1)
+    out_done(1)
+    grad[0].pump(0)
     lax.fori_loop(0, 8, qkv_back, 1)
-    out_done(0)
-    out_done(1)
     grad[1].produce(0)
-    grad[0].produce(0)
+    grad[1].produce(1)
     grad[1].pump(0)
-    grad[0].produce(1)
-    grad[0].pump(0)
-    grad[1].produce(1)
     grad[0].produce(2)
-    grad[0].produce(3)
-    grad[1].pump(1)
     grad[0].pump(1)
     grad[1].produce(2)
-    grad[1].pump(2)
+    grad[1].pump(1)
     grad[1].produce(3)
+    grad[0].produce(3)
     qkv_weights()
     grad[0].pump(2)
+    grad[1].pump(2)
+    pd_weights()
+    dm.start()
+    grad[0].pump(3)
+    token_sums()
     grad[1].pump(3)
-    pd_weights()
-    grad[0].pump(3)
     weights_out(0)
+    grad_done(1)
     grad_done(0)
-    token_sums()
-    grad_done(1)
 
     for e in range(2):
         @pl.when(jnp.logical_not(here & (d == e)))

time: 132 us -> 130 us (0.985)
  Pallas kernels: 131 us -> 129 us
    pallas_call x1, Pallas kernels: 128 us -> 126 us  [fast_shards(): pl.pallas_call(block_kernel, out_shape=(sds((128, D), bf16), sds((128, D)...]
where the time goes in v4:
time: 130 us
  Pallas kernels  129 us (99%)
    pallas_call x1, Pallas kernels, fast_shards(): pl.pallas_call(block_kernel, out_shape=(sds((128, D), bf16), sds((128, D)...  126 us
    pallas_call x1, Pallas kernels, fast_shards(): pl.pallas_call(finish_kernel, out_shape=(sds((2, 64, D), bf16), sds((2, 6...  3.19 us

profile of v4, /device:TPU:0, one launch (start us, length us, event | category | flops | bytes accessed | tf_op | source)
XLA Modules:
  0.0 129.9 jit_solution(442402432685076996)
XLA Ops:
  0.7 126.1 %shard_map.271 = (bf16[128,1024]{1,0:T(8,128)(2,1)}, bf16[128,1024]{1,0:T(8,128)(2,1)}, bf16[16,32,256]{2,1,0:T(8,128)(2,1)}, bf16[16,32,256]{2,1,0:T(8,128)(2,1...) custom-call(s32[16]{0:T(128)} %go_ref.1, s32[2,4]{1,0:T(2,128)} %ps_ref.1, ...), custom_call_target="tpu_custom_call" | custom-call | tf_op jit(solution)/shard_map/pallas_call | solution.py:1240
  126.7 3.2 %shard_map.272 = (bf16[2,64,1024]{2,1,0:T(8,128)(2,1)}, bf16[2,64,1024]{2,1,0:T(8,128)(2,1)}, f32[1,32]{1,0:T(1,128)}, f32[1,32]{1,0:T(1,128)}, f32[32,3072]{1,0...) custom-call(bf16[128,1024]{1,0:T(8,128)(2,1)} %get-tuple-element.37., ...), custom_call_target="tpu_custom_call" | custom-call | tf_op jit(solution)/shard_map/pallas_call | solution.py:1278

commit v5 on v4

--- a/solution.py
+++ b/solution.py
@@ -657,9 +657,12 @@
         wy_copy(o, d).start()
         return 0
 
-    lax.fori_loop(1, NC, w_wait, 0)
+    lax.fori_loop(1, 6, w_wait, 0)
+    gx[0].pump(1)
+    lax.fori_loop(6, 11, w_wait, 0)
+    gx[1].pump(1)
+    lax.fori_loop(11, NC, w_wait, 0)
     pd_start()
-    gx[0].pump(1)
 
     def wy_wait(o, _):
         wy_copy(o, 1 - d).wait_recv()
@@ -1015,7 +1018,6 @@
                      - nrm * jnp.mean(tot * nrm, axis=1, keepdims=True))
         ).astype(bf16)
 
-    gx[1].pump(1)
     gx[0].pump(2)
     n_blocks(1, 0)
     n_blocks(0, 1)

time: 130 us -> 127 us (0.977)
  Pallas kernels: 129 us -> 126 us
    pallas_call x1, Pallas kernels: 126 us -> 123 us  [fast_shards(): pl.pallas_call(block_kernel, out_shape=(sds((128, D), bf16), sds((128, D)...]
where the time goes in v5:
time: 127 us
  Pallas kernels  126 us (99%)
    pallas_call x1, Pallas kernels, fast_shards(): pl.pallas_call(block_kernel, out_shape=(sds((128, D), bf16), sds((128, D)...  123 us
    pallas_call x1, Pallas kernels, fast_shards(): pl.pallas_call(finish_kernel, out_shape=(sds((2, 64, D), bf16), sds((2, 6...  3.19 us

profile of v5, /device:TPU:0, one launch (start us, length us, event | category | flops | bytes accessed | tf_op | source)
XLA Modules:
  0.0 127.0 jit_solution(802565107202969779)
XLA Ops:
  0.7 123.2 %shard_map.271 = (bf16[128,1024]{1,0:T(8,128)(2,1)}, bf16[128,1024]{1,0:T(8,128)(2,1)}, bf16[16,32,256]{2,1,0:T(8,128)(2,1)}, bf16[16,32,256]{2,1,0:T(8,128)(2,1...) custom-call(s32[16]{0:T(128)} %go_ref.1, s32[2,4]{1,0:T(2,128)} %ps_ref.1, ...), custom_call_target="tpu_custom_call" | custom-call | tf_op jit(solution)/shard_map/pallas_call | solution.py:1242
  123.8 3.2 %shard_map.272 = (bf16[2,64,1024]{2,1,0:T(8,128)(2,1)}, bf16[2,64,1024]{2,1,0:T(8,128)(2,1)}, f32[1,32]{1,0:T(1,128)}, f32[1,32]{1,0:T(1,128)}, f32[32,3072]{1,0...) custom-call(bf16[128,1024]{1,0:T(8,128)(2,1)} %get-tuple-element.37., ...), custom_call_target="tpu_custom_call" | custom-call | tf_op jit(solution)/shard_map/pallas_call | solution.py:1280
